TPU v7x, 512 devices: a whole 4x4x16 slice. The times are simulated.
512 devices in a mesh: gx: 8 (over y, core), gy: 8 (over x, z_hi), gz: 8 (over z_lo).
Axes of the slice: x: 4, y: 4, z: 16 (z_hi: 2, z_lo: 8; z = z_hi * 8 + z_lo), core: 2. Of those that a mesh axis runs over, the one named last changes fastest.
Arguments:
- loads: float32 [8, 3, 32, 64, 1024], P(None, None, 'gx', 'gy', 'gz'), may hold values from -6 to 6
- iterate: float32 [8, 3, 32, 64, 1024], P(None, None, 'gx', 'gy', 'gz'), may hold values from -4 to 4
- classes: int32 [32, 64, 1024], P('gx', 'gy', 'gz'), may hold values from 0 to 7
- stiffness: float32 [8], replicated, may hold values from 0.5 to 5
- density: float32 [8], replicated, may hold values from 1 to 4
- basis: float32 [32, 3, 32, 64, 1024], P(None, None, 'gx', 'gy', 'gz'), may hold values from -0.625 to 0.625
- coarse_inverse: float32 [16384, 16384], P(('gx', 'gy', 'gz')), may hold values from -0.046875 to 0.046875
Outputs:
- updated: float32 [8, 3, 32, 64, 1024], P(None, None, 'gx', 'gy', 'gz')
All inputs are finite; a program needn't handle non-finite values.
Results may differ from a plain program's by a relative error of at most 0.0003.
Values sent between devices are 32-bit elements; how exact they have to be, the bound alone decides.
A program may use at most 64 MiB of HBM per device.

v0:
```python
import jax
import jax.numpy as jnp
from jax import lax
from jax.sharding import PartitionSpec as P

SWEEPS = 4


coupling = 0.1
damping = 0.7


def extended(block, sides, width):
    for axis, dim in sides:
        count = lax.axis_size(axis)
        forward = [(i, i + 1) for i in range(count - 1)]
        backward = [(target, source) for source, target in forward]
        low = lax.ppermute(
            lax.slice_in_dim(block, block.shape[dim] - width, None, axis=dim), axis, forward
        )
        high = lax.ppermute(lax.slice_in_dim(block, 0, width, axis=dim), axis, backward)
        block = jnp.concatenate([low, block, high], axis=dim)
    return block


def lookup(classes, table):
    matches = classes[..., None] == jnp.arange(table.shape[0], dtype=jnp.int32)
    return jnp.sum(jnp.where(matches, table, jnp.float32(0.0)), axis=-1)


def stencil(padded, stiff_field, mass_field):
    center = padded[..., 1:-1, 1:-1, 1:-1]
    beside = padded[..., 2:, 1:-1, 1:-1] + padded[..., :-2, 1:-1, 1:-1]
    beside = beside + padded[..., 1:-1, 2:, 1:-1] + padded[..., 1:-1, :-2, 1:-1]
    beside = beside + padded[..., 1:-1, 1:-1, 2:] + padded[..., 1:-1, 1:-1, :-2]
    summed = jnp.sum(center, axis=1, keepdims=True)
    return (
        (6.0 * stiff_field + mass_field) * center
        - stiff_field * beside
        + coupling * stiff_field * (summed - center)
    )


def smooth(residual_ext, shifted_classes, stiffness, density):
    inside = shifted_classes > 0
    material = shifted_classes - 1
    stiff_field = lookup(material, stiffness)
    mass_field = lookup(material, density)
    diagonal = jnp.where(
        inside, 6.0 * stiff_field + mass_field - coupling * stiff_field, jnp.float32(1.0)
    )
    update = jnp.zeros_like(residual_ext)
    for sweep in range(SWEEPS):
        padded = jnp.pad(update, ((0, 0), (0, 0), (1, 1), (1, 1), (1, 1)))
        update = jnp.where(
            inside,
            update + damping * (residual_ext - stencil(padded, stiff_field, mass_field)) / diagonal,
            jnp.float32(0.0),
        )
    return update[..., 2:-2, 2:-2, 2:-2]


def shards(loads, iterate, classes, stiffness, density, basis, coarse_inverse):
    highest = lax.Precision.HIGHEST
    shifted = extended(classes + 1, (("gx", 0), ("gy", 1), ("gz", 2)), 2)
    stiff_field = lookup(classes, stiffness)
    mass_field = lookup(classes, density)
    padded = extended(iterate, (("gx", 2), ("gy", 3), ("gz", 4)), 1)
    residual = loads - stencil(padded, stiff_field, mass_field)
    residual_ext = extended(residual, (("gx", 2), ("gy", 3), ("gz", 4)), 2)
    fine = smooth(residual_ext, shifted, stiffness, density)
    flat_basis = basis.reshape(basis.shape[0], -1)
    coeff = jnp.dot(flat_basis, residual.reshape(residual.shape[0], -1).T, precision=highest)
    solved = jnp.dot(
        coarse_inverse,
        lax.all_gather(coeff, ("gx", "gy", "gz"), axis=0, tiled=True),
        precision=highest,
    )
    correction = jnp.dot(solved.T, flat_basis, precision=highest).reshape(iterate.shape)
    return iterate + fine + correction


def solution(mesh):
    placed = (
        P(None, None, "gx", "gy", "gz"),
        P(None, None, "gx", "gy", "gz"),
        P("gx", "gy", "gz"),
        P(),
        P(),
        P(None, None, "gx", "gy", "gz"),
        P(("gx", "gy", "gz"), None),
    )
    return jax.shard_map(
        shards,
        mesh=mesh,
        in_specs=placed,
        out_specs=P(None, None, "gx", "gy", "gz"),
        check_vma=False,
    )
```

profile of v0, /device:TPU:32, one launch (start us, length us, event | category | flops | bytes accessed | tf_op | source)
XLA Modules:
  0.0 311.9 jit_solution(5241280569334992297)
XLA Ops:
  5.2 4.4 %collective-permute-start.7 = (f32[8,3,1,8,128]{4,0,3,2,1:T(8,128)S(1)}, f32[8,3,1,8,128]{4,0,3,2,1:T(8,128)S(1)}, u32[]{:S(2)}, u32[]{:S(2)}) collective-permute-start(f32[8,3,1,8,128]{4,0,3,2,1:T(8,128)S(1)} %get-tuple-element.33), channel_id=1, source_target_pairs={{0,64},{64,128},{128,192},{192,256},{256,320},{320,384},{384,448},... | collective-permute-start | bytes 294920 | tf_op jit(solution)/shard_map/ppermute | solution.py:18
  10.9 14.8 %collective-permute-start.2 = (s32[8,2,128]{2,1,0:T(2,128)S(1)}, s32[8,2,128]{2,1,0:T(2,128)S(1)}, u32[]{:S(2)}, u32[]{:S(2)}) collective-permute-start(s32[8,2,128]{2,1,0:T(2,128)S(1)} %get-tuple-element.38), channel_id=1, source_target_pairs={{0,8},{8,16},{16,24},{24,32},{32,40},{40,48},{48,56},{1,9},{9,17},... | collective-permute-start | bytes 24584 | tf_op jit(solution)/shard_map/ppermute | solution.py:18
  28.0 12.1 %collective-permute-done.3 = s32[8,2,128]{2,1,0:T(2,128)S(1)} collective-permute-done((s32[8,2,128]{2,1,0:T(2,128)S(1)}, s32[8,2,128]{2,1,0:T(2,128)S(1)}, u32[]{:S(2)}, u32[]{:S(2)}) %collective-permute-start.3) | collective-permute-done | bytes 8224 | tf_op jit(solution)/shard_map/ppermute | solution.py:21
  40.1 2.9 collective-permute-start.4
  43.1 2.9 collective-permute-start.5
  48.4 2.3 copy.92
  54.1 13.3 %collective-permute-start.9 = (f32[8,3,6,1,128]{4,0,3,2,1:T(8,128)S(1)}, f32[8,3,6,1,128]{4,0,3,2,1:T(8,128)S(1)}, u32[]{:S(2)}, u32[]{:S(2)}) collective-permute-start(f32[8,3,6,1,128]{4,0,3,2,1:T(8,128)S(1)} %get-tuple-element.28), channel_id=1, source_target_pairs={{0,8},{8,16},{16,24},{24,32},{32,40},{40,48},{48,56},{1,9},{9,17},... | collective-permute-start | bytes 221192 | tf_op jit(solution)/shard_map/ppermute | solution.py:18
  68.6 6.4 %collective-permute-done.8 = f32[8,3,6,1,128]{4,0,3,2,1:T(8,128)S(1)} collective-permute-done((f32[8,3,6,1,128]{4,0,3,2,1:T(8,128)S(1)}, f32[8,3,6,1,128]{4,0,3,2,1:T(8,128)S(1)}, u32[]{:S(2)}, u32[]{:S(2)}) %collective-permute-start.8) | collective-permute-done | bytes 73760 | tf_op jit(solution)/shard_map/ppermute | solution.py:21
  77.4 2.7 copy.60
  83.6 4.0 %collective-permute-start.11 = (f32[8,3,6,10,1]{3,0,4,2,1:T(8,128)}, f32[8,3,6,10,1]{3,0,4,2,1:T(8,128)S(1)}, u32[]{:S(2)}, u32[]{:S(2)}) collective-permute-start(f32[8,3,6,10,1]{3,0,4,2,1:T(8,128)} %copy.62), channel_id=1, source_target_pairs={{0,1},{1,2},{2,3},{3,4},{4,5},{5,6},{6,7},{8,9},{9,10},{10,11},{11... | collective-permute-start | bytes 17288 | tf_op jit(solution)/shard_map/ppermute | solution.py:18
  89.2 2.7 copy.61
  93.8 2.4 fusion.63
  102.8 12.2 %collective-permute-start.14 = (f32[8,3,8,2,128]{4,0,3,2,1:T(8,128)}, f32[8,3,8,2,128]{4,0,3,2,1:T(8,128)}, u32[]{:S(2)}, u32[]{:S(2)}) collective-permute-start(f32[8,3,8,2,128]{4,0,3,2,1:T(8,128)} %get-tuple-element.24), channel_id=1, source_target_pairs={{0,8},{8,16},{16,24},{24,32},{32,40},{40,48},{48,56},{1,9},{9,17},... | collective-permute-start | bytes 589832 | tf_op jit(solution)/shard_map/ppermute | solution.py:18
  116.4 147.5 %all-gather = f32[512,32,8]{1,2,0:T(8,128)S(1)} all-gather(f32[1,32,8]{1,2,0:T(8,128)S(1)} %fusion.52), channel_id=1, replica_groups=mesh['gx'=8,'gy'=8,'gz'=8] {'gx','gy','gz'}, dimensions={0}, use_global_device_ids=true | all-gather | bytes 525312 | tf_op jit(solution)/shard_map/all_gather | solution.py:76
  265.6 3.4 %reshape.83 = f32[16384,8]{0,1:T(8,128)} reshape(f32[512,32,8]{1,0,2:T(8,128)} %copy.73) | data formatting | bytes 1048576
  272.1 3.2 %copy.67 = f32[8,3,8,12,2]{3,2,4,1,0:T(8,128)} copy(f32[8,3,8,12,2]{4,0,3,2,1:T(8,128)} %get-tuple-element.22) | data formatting | bytes 36864 | tf_op jit(solution)/shard_map/slice | solution.py:19
  277.5 3.2 %copy.68 = f32[8,3,8,12,2]{3,2,4,1,0:T(8,128)} copy(f32[8,3,8,12,2]{4,0,3,2,1:T(8,128)} %get-tuple-element.23) | data formatting | bytes 36864 | tf_op jit(solution)/shard_map/slice | solution.py:21
  280.7 4.3 %collective-permute-start.17 = (f32[8,3,8,12,2]{3,2,4,1,0:T(8,128)}, f32[8,3,8,12,2]{3,2,4,1,0:T(8,128)}, u32[]{:S(2)}, u32[]{:S(2)}) collective-permute-start(f32[8,3,8,12,2]{3,2,4,1,0:T(8,128)} %copy.68), channel_id=1, source_target_pairs={{1,0},{2,1},{3,2},{4,3},{5,4},{6,5},{7,6},{9,8},{10,9},{11,10},{12... | collective-permute-start | bytes 55304 | tf_op jit(solution)/shard_map/ppermute | solution.py:21
  285.0 2.8 convolution_bitcast_fusion
  287.7 3.2 %copy.69 = f32[8,3,8,12,2]{4,0,3,2,1:T(8,128)} copy(f32[8,3,8,12,2]{3,2,4,1,0:T(8,128)} %collective-permute-done.16) | data formatting | bytes 36864 | tf_op jit(solution)/shard_map/ppermute | solution.py:18
  291.0 3.2 %copy.70 = f32[8,3,8,12,2]{4,0,3,2,1:T(8,128)} copy(f32[8,3,8,12,2]{3,2,4,1,0:T(8,128)} %collective-permute-done.17) | data formatting | bytes 36864 | tf_op jit(solution)/shard_map/ppermute | solution.py:21
  295.8 5.0 %fusion.72 = (f32[8,8,12,132]{3,0,2,1:T(8,128)S(1)}, f32[8,3,8,12,132]{4,0,3,2,1:T(8,128)S(1)}, f32[8,3,8,12,132]{4,0,3,2,1:T(8,128)S(1)}) fusion(f32[8,3,8,12,132]{4,0,3,2,1:T(8,128)S(1)} %broadcast_in_dim.85, f32[8,12,132]{2,1,0:T(8,128)S(1)} %get-tuple-element.18, f32[8,12,132]{2,1,0:T(8,128)} %get-tuple-element.35, ...), kind=kLoop, calls=%fused_computation.136 | loop fusion | flops 5677056 | bytes 5486976 | tf_op jit(solution)/shard_map/reduce_sum | solution.py:36
  300.8 2.9 fusion.70
  303.8 3.0 fusion.68
  (122 shorter events, 46.5 us)
Async XLA Ops:
  0.0 285.0 %copy-start = (f32[32,16384]{1,0:T(8,128)S(1)}, f32[32,16384]{1,0:T(8,128)}, u32[]{:S(2)}) copy-start(f32[32,16384]{1,0:T(8,128)} %param.13) | copy-start | bytes 6291460
  0.9 10.0 %collective-permute-start = (s32[2,8,128]{2,1,0:T(8,128)S(1)}, s32[2,8,128]{2,1,0:T(8,128)S(1)}, u32[]{:S(2)}, u32[]{:S(2)}) collective-permute-start(s32[2,8,128]{2,1,0:T(8,128)S(1)} %get-tuple-element.40), channel_id=1, source_target_pairs={{0,64},{64,128},{128,192},{192,256},{256,320},{320,384},{384,448},... | collective-permute-start | bytes 24584 | tf_op jit(solution)/shard_map/ppermute | solution.py:18
  2.6 8.3 %collective-permute-start.1 = (s32[2,8,128]{2,1,0:T(8,128)S(1)}, s32[2,8,128]{2,1,0:T(8,128)S(1)}, u32[]{:S(2)}, u32[]{:S(2)}) collective-permute-start(s32[2,8,128]{2,1,0:T(8,128)S(1)} %get-tuple-element.41), channel_id=1, source_target_pairs={{64,0},{128,64},{192,128},{256,192},{320,256},{384,320},{448,384},... | collective-permute-start | bytes 24584 | tf_op jit(solution)/shard_map/ppermute | solution.py:21
  5.1 43.2 %copy-start.7 = (f32[8,3,4,8,128]{4,0,3,2,1:T(8,128)}, f32[8,3,4,8,128]{4,0,3,2,1:T(8,128)S(1)}, u32[]{:S(2)}) copy-start(f32[8,3,4,8,128]{4,0,3,2,1:T(8,128)S(1)} %copy.71) | copy-start | bytes 1179652
  5.2 47.2 %collective-permute-start.7 = (f32[8,3,1,8,128]{4,0,3,2,1:T(8,128)S(1)}, f32[8,3,1,8,128]{4,0,3,2,1:T(8,128)S(1)}, u32[]{:S(2)}, u32[]{:S(2)}) collective-permute-start(f32[8,3,1,8,128]{4,0,3,2,1:T(8,128)S(1)} %get-tuple-element.33), channel_id=1, source_target_pairs={{0,64},{64,128},{128,192},{192,256},{256,320},{320,384},{384,448},... | collective-permute-start | bytes 294920 | tf_op jit(solution)/shard_map/ppermute | solution.py:18
  9.6 43.1 %collective-permute-start.6 = (f32[8,3,1,8,128]{4,0,3,2,1:T(8,128)S(1)}, f32[8,3,1,8,128]{4,0,3,2,1:T(8,128)S(1)}, u32[]{:S(2)}, u32[]{:S(2)}) collective-permute-start(f32[8,3,1,8,128]{4,0,3,2,1:T(8,128)S(1)} %get-tuple-element.32), channel_id=1, source_target_pairs={{64,0},{128,64},{192,128},{256,192},{320,256},{384,320},{448,384},... | collective-permute-start | bytes 294920 | tf_op jit(solution)/shard_map/ppermute | solution.py:21
  10.9 41.3 %copy-start.20 = (s32[2,8,128]{2,1,0:T(8,128)}, s32[2,8,128]{2,1,0:T(8,128)S(1)}, u32[]{:S(2)}) copy-start(s32[2,8,128]{2,1,0:T(8,128)S(1)} %collective-permute-done) | copy-start | bytes 24580
  10.9 41.3 %copy-start.22 = (s32[2,8,128]{2,1,0:T(8,128)}, s32[2,8,128]{2,1,0:T(8,128)S(1)}, u32[]{:S(2)}) copy-start(s32[2,8,128]{2,1,0:T(8,128)S(1)} %collective-permute-done.1) | copy-start | bytes 24580
  10.9 17.0 %collective-permute-start.2 = (s32[8,2,128]{2,1,0:T(2,128)S(1)}, s32[8,2,128]{2,1,0:T(2,128)S(1)}, u32[]{:S(2)}, u32[]{:S(2)}) collective-permute-start(s32[8,2,128]{2,1,0:T(2,128)S(1)} %get-tuple-element.38), channel_id=1, source_target_pairs={{0,8},{8,16},{16,24},{24,32},{32,40},{40,48},{48,56},{1,9},{9,17},... | collective-permute-start | bytes 24584 | tf_op jit(solution)/shard_map/ppermute | solution.py:18
  25.8 14.3 %collective-permute-start.3 = (s32[8,2,128]{2,1,0:T(2,128)S(1)}, s32[8,2,128]{2,1,0:T(2,128)S(1)}, u32[]{:S(2)}, u32[]{:S(2)}) collective-permute-start(s32[8,2,128]{2,1,0:T(2,128)S(1)} %get-tuple-element.39), channel_id=1, source_target_pairs={{8,0},{16,8},{24,16},{32,24},{40,32},{48,40},{56,48},{9,1},{17,9},... | collective-permute-start | bytes 24584 | tf_op jit(solution)/shard_map/ppermute | solution.py:21
  28.0 24.3 %copy-start.24 = (s32[8,2,128]{2,1,0:T(2,128)}, s32[8,2,128]{2,1,0:T(2,128)S(1)}, u32[]{:S(2)}) copy-start(s32[8,2,128]{2,1,0:T(2,128)S(1)} %collective-permute-done.2) | copy-start | bytes 24580
  40.1 12.1 %collective-permute-start.4 = (s32[8,12,2]{2,1,0:T(8,128)S(1)}, s32[8,12,2]{2,1,0:T(8,128)S(1)}, u32[]{:S(2)}, u32[]{:S(2)}) collective-permute-start(s32[8,12,2]{2,1,0:T(8,128)S(1)} %get-tuple-element.36), channel_id=1, source_target_pairs={{0,1},{1,2},{2,3},{3,4},{4,5},{5,6},{6,7},{8,9},{9,10},{10,11},{11... | collective-permute-start | bytes 2312 | tf_op jit(solution)/shard_map/ppermute | solution.py:18
  43.1 9.1 %collective-permute-start.5 = (s32[8,12,2]{2,1,0:T(8,128)S(1)}, s32[8,12,2]{2,1,0:T(8,128)S(1)}, u32[]{:S(2)}, u32[]{:S(2)}) collective-permute-start(s32[8,12,2]{2,1,0:T(8,128)S(1)} %get-tuple-element.37), channel_id=1, source_target_pairs={{1,0},{2,1},{3,2},{4,3},{5,4},{6,5},{7,6},{9,8},{10,9},{11,10},{12... | collective-permute-start | bytes 2312 | tf_op jit(solution)/shard_map/ppermute | solution.py:21
  52.4 22.7 %copy-start.11 = (f32[8,3,1,8,128]{4,0,3,2,1:T(8,128)}, f32[8,3,1,8,128]{4,0,3,2,1:T(8,128)S(1)}, u32[]{:S(2)}) copy-start(f32[8,3,1,8,128]{4,0,3,2,1:T(8,128)S(1)} %collective-permute-done.7) | copy-start | bytes 294916
  52.9 22.2 %collective-permute-start.8 = (f32[8,3,6,1,128]{4,0,3,2,1:T(8,128)S(1)}, f32[8,3,6,1,128]{4,0,3,2,1:T(8,128)S(1)}, u32[]{:S(2)}, u32[]{:S(2)}) collective-permute-start(f32[8,3,6,1,128]{4,0,3,2,1:T(8,128)S(1)} %get-tuple-element.29), channel_id=1, source_target_pairs={{8,0},{16,8},{24,16},{32,24},{40,32},{48,40},{56,48},{9,1},{17,9},... | collective-permute-start | bytes 221192 | tf_op jit(solution)/shard_map/ppermute | solution.py:21
  54.1 20.9 %collective-permute-start.9 = (f32[8,3,6,1,128]{4,0,3,2,1:T(8,128)S(1)}, f32[8,3,6,1,128]{4,0,3,2,1:T(8,128)S(1)}, u32[]{:S(2)}, u32[]{:S(2)}) collective-permute-start(f32[8,3,6,1,128]{4,0,3,2,1:T(8,128)S(1)} %get-tuple-element.28), channel_id=1, source_target_pairs={{0,8},{8,16},{16,24},{24,32},{32,40},{40,48},{48,56},{1,9},{9,17},... | collective-permute-start | bytes 221192 | tf_op jit(solution)/shard_map/ppermute | solution.py:18
  80.1 9.1 %collective-permute-start.10 = (f32[8,3,6,10,1]{3,0,4,2,1:T(8,128)}, f32[8,3,6,10,1]{3,0,4,2,1:T(8,128)}, u32[]{:S(2)}, u32[]{:S(2)}) collective-permute-start(f32[8,3,6,10,1]{3,0,4,2,1:T(8,128)} %copy.60), channel_id=1, source_target_pairs={{1,0},{2,1},{3,2},{4,3},{5,4},{6,5},{7,6},{9,8},{10,9},{11,10},{12... | collective-permute-start | bytes 17288 | tf_op jit(solution)/shard_map/ppermute | solution.py:21
  83.6 8.3 %collective-permute-start.11 = (f32[8,3,6,10,1]{3,0,4,2,1:T(8,128)}, f32[8,3,6,10,1]{3,0,4,2,1:T(8,128)S(1)}, u32[]{:S(2)}, u32[]{:S(2)}) collective-permute-start(f32[8,3,6,10,1]{3,0,4,2,1:T(8,128)} %copy.62), channel_id=1, source_target_pairs={{0,1},{1,2},{2,3},{3,4},{4,5},{5,6},{6,7},{8,9},{9,10},{10,11},{11... | collective-permute-start | bytes 17288 | tf_op jit(solution)/shard_map/ppermute | solution.py:18
  96.3 5.6 %collective-permute-start.12 = (f32[8,3,2,8,128]{4,0,3,2,1:T(8,128)S(1)}, f32[8,3,2,8,128]{4,0,3,2,1:T(8,128)S(1)}, u32[]{:S(2)}, u32[]{:S(2)}) collective-permute-start(f32[8,3,2,8,128]{4,0,3,2,1:T(8,128)S(1)} %get-tuple-element.30), channel_id=1, source_target_pairs={{0,64},{64,128},{128,192},{192,256},{256,320},{320,384},{384,448},... | collective-permute-start | bytes 589832 | tf_op jit(solution)/shard_map/ppermute | solution.py:18
  97.6 4.4 %collective-permute-start.13 = (f32[8,3,2,8,128]{4,0,3,2,1:T(8,128)S(1)}, f32[8,3,2,8,128]{4,0,3,2,1:T(8,128)S(1)}, u32[]{:S(2)}, u32[]{:S(2)}) collective-permute-start(f32[8,3,2,8,128]{4,0,3,2,1:T(8,128)S(1)} %get-tuple-element.31), channel_id=1, source_target_pairs={{64,0},{128,64},{192,128},{256,192},{320,256},{384,320},{448,384},... | collective-permute-start | bytes 589832 | tf_op jit(solution)/shard_map/ppermute | solution.py:21
  102.8 166.1 %collective-permute-start.14 = (f32[8,3,8,2,128]{4,0,3,2,1:T(8,128)}, f32[8,3,8,2,128]{4,0,3,2,1:T(8,128)}, u32[]{:S(2)}, u32[]{:S(2)}) collective-permute-start(f32[8,3,8,2,128]{4,0,3,2,1:T(8,128)} %get-tuple-element.24), channel_id=1, source_target_pairs={{0,8},{8,16},{16,24},{24,32},{32,40},{40,48},{48,56},{1,9},{9,17},... | collective-permute-start | bytes 589832 | tf_op jit(solution)/shard_map/ppermute | solution.py:18
  115.1 153.9 %collective-permute-start.15 = (f32[8,3,8,2,128]{4,0,3,2,1:T(8,128)}, f32[8,3,8,2,128]{4,0,3,2,1:T(8,128)}, u32[]{:S(2)}, u32[]{:S(2)}) collective-permute-start(f32[8,3,8,2,128]{4,0,3,2,1:T(8,128)} %get-tuple-element.25), channel_id=1, source_target_pairs={{8,0},{16,8},{24,16},{32,24},{40,32},{48,40},{56,48},{9,1},{17,9},... | collective-permute-start | bytes 589832 | tf_op jit(solution)/shard_map/ppermute | solution.py:21
  275.3 12.4 %collective-permute-start.16 = (f32[8,3,8,12,2]{3,2,4,1,0:T(8,128)}, f32[8,3,8,12,2]{3,2,4,1,0:T(8,128)}, u32[]{:S(2)}, u32[]{:S(2)}) collective-permute-start(f32[8,3,8,12,2]{3,2,4,1,0:T(8,128)} %copy.67), channel_id=1, source_target_pairs={{0,1},{1,2},{2,3},{3,4},{4,5},{5,6},{6,7},{8,9},{9,10},{10,11},{11... | collective-permute-start | bytes 55304 | tf_op jit(solution)/shard_map/ppermute | solution.py:18
  280.7 10.3 %collective-permute-start.17 = (f32[8,3,8,12,2]{3,2,4,1,0:T(8,128)}, f32[8,3,8,12,2]{3,2,4,1,0:T(8,128)}, u32[]{:S(2)}, u32[]{:S(2)}) collective-permute-start(f32[8,3,8,12,2]{3,2,4,1,0:T(8,128)} %copy.68), channel_id=1, source_target_pairs={{1,0},{2,1},{3,2},{4,3},{5,4},{6,5},{7,6},{9,8},{10,9},{11,10},{12... | collective-permute-start | bytes 55304 | tf_op jit(solution)/shard_map/ppermute | solution.py:21
  (24 other events, 192.5 us)
where the time goes:
time: 313 us; the launch traced here: 312 us
  blocking collectives  148 us (47%)
  starting transfers between devices  73.7 us (24%)
  local copies, waits for them, and re-layouts  39.7 us (13%)
  other arithmetic  24.8 us (8%)
  waiting for transfers between devices  18.7 us (6%)
  matrix products  6.84 us (2%)
    all_gather x1, blocking collectives, shards(): lax.all_gather(coeff, ('gx', 'gy', 'gz'), axis=0, tiled=True)  148 us
    ppermute x9, starting transfers between devices, extended(): lax.ppermute(lax.slice_in_dim(block, block.shape[dim] - width, None, axis...  56.9 us
    ppermute x9, waiting for transfers between devices, extended(): lax.ppermute(lax.slice_in_dim(block, 0, width, axis=dim), axis, backward)  18.7 us
    ppermute x9, starting transfers between devices, extended(): lax.ppermute(lax.slice_in_dim(block, 0, width, axis=dim), axis, backward)  16.8 us
    reduce_sum x4, other arithmetic, stencil(): summed = jnp.sum(center, axis=1, keepdims=True)  11.9 us
    unnamed x66, local copies, waits for them, and re-layouts  11.4 us
    slice x4, local copies, waits for them, and re-layouts, extended(): lax.slice_in_dim(block, 0, width, axis=dim)  6.93 us
    slice x7, local copies, waits for them, and re-layouts, extended(): lax.slice_in_dim(block, block.shape[dim] - width, None, axis=dim)  6.71 us
  transfers between devices with their start and end apart: 18, of which 3 were waited for; matrix products, arithmetic and copies ran while one was open for 11% of the time, Pallas kernels for 0%

commit v1 on v0

v1 whole, which is shorter than its diff:
```python
import functools

import jax
import jax.numpy as jnp
from jax import lax
from jax.experimental import pallas as pl
from jax.experimental.pallas import tpu as pltpu
from jax.sharding import PartitionSpec as P

MESH = pl.DeviceIdType.MESH
F32, BF16, I32 = jnp.float32, jnp.bfloat16, jnp.int32
FIELDS = 24
CHUNKS, PER = 4, 6
COUPLING, DAMPING = 0.1, 0.7
NT = (((1,), (1,)), ((), ()))


def lookup(classes, table):
    found = jnp.zeros(classes.shape, F32)
    for k in range(8):
        found = found + jnp.where(classes == k, table[k], 0.0)
    return found


def halves(v):
    high = v.astype(BF16)
    return high, (v - high.astype(F32)).astype(BF16)


def iota(shape, axis):
    return lax.broadcasted_iota(I32, shape, axis)


def beside_x(v, axis):
    row = iota(v.shape, axis)
    return jnp.where(row == 0, 0.0, pltpu.roll(v, 1, axis)) + jnp.where(row == 7, 0.0, pltpu.roll(v, 7, axis))


def kernel(
    ny, nx, nz, loads, iterate, classes, stiffness, density, basis, cinv, out,
    it, ld, acc, cls, bas, ci, res, iys, iyr, ixs, ixr, izs, izr, cbox, czs, czr, box, ys, yr,
    zs, zr, bt, c2, g1, g2, sbox, wbox, bbox, zw, zb, ga, gb, gc, za, zc, zd, vy,
    ss, rs, ls,
):
    gx, gy, gz = lax.axis_index("gx"), lax.axis_index("gy"), lax.axis_index("gz")
    half = nz // 2
    py, core, px, pz = gx // 2, gx % 2, gy // 2, (gy % 2) * half + gz

    def chip(x, y, z, c):
        return (y * 2 + c, x * 2 + z // half, z % half)

    steps = {
        "gx": ((gx - 1, gy, gz), gx > 0, (gx + 1, gy, gz), gx < 2 * ny - 1),
        "gy": ((gx, gy - 1, gz), gy > 0, (gx, gy + 1, gz), gy < 2 * nx - 1),
        "gz": ((gx, gy, gz - 1), gz > 0, (gx, gy, gz + 1), gz < half - 1),
    }
    count = [0]
    pending = []

    def exchange(axis, low_src, low_dst, high_src, high_dst):
        lower, has_lower, upper, has_upper = steps[axis]
        i = count[0]
        count[0] += 2
        down = pltpu.make_async_remote_copy(low_src, low_dst, ss.at[i], rs.at[i], lower, MESH)
        up = pltpu.make_async_remote_copy(high_src, high_dst, ss.at[i + 1], rs.at[i + 1], upper, MESH)
        pl.when(has_lower)(down.start)
        pl.when(has_upper)(up.start)

        def sent():
            pl.when(has_lower)(down.wait_send)
            pl.when(has_upper)(up.wait_send)

        def arrived():
            pl.when(has_upper)(down.wait_recv)
            pl.when(has_lower)(up.wait_recv)

        pending.append(sent)
        return arrived

    local = [
        pltpu.make_async_copy(a, b, ls.at[i])
        for i, (a, b) in enumerate(((iterate, it), (classes, cls), (loads, ld), (basis, bas), (cinv, ci)))
    ]
    for copy in local:
        copy.start()

    for ref in (iyr, ixr, izr, cbox, czr, box, yr, zr):
        ref[...] = jnp.zeros(ref.shape, ref.dtype)

    barrier = pltpu.get_barrier_semaphore()
    high_half = gy % 2
    across_gx = jnp.where(core == 1, gx < 2 * ny - 1, gx > 0)
    across_gy = jnp.where(high_half == 1, gy < 2 * nx - 1, gy > 0)
    for there, to in ((across_gx, (gx + 2 * core - 1, gy, gz)), (across_gy, (gx, gy + 2 * high_half - 1, gz))):
        pl.when(there)(functools.partial(pl.semaphore_signal, barrier, inc=1, device_id=to, device_id_type=MESH))

    def greet_line(k, carry):
        pl.semaphore_signal(barrier, inc=1, device_id=chip(px, py, lax.rem(pz + k, nz), core), device_id_type=MESH)
        return carry

    lax.fori_loop(1, nz, greet_line, 0)

    def other(p, sign):
        dx, dy = p // ny, lax.rem(p, ny)
        return lax.rem(px + sign * dx + nx, nx), lax.rem(py + sign * dy + ny, ny)

    def greet_plane(p, carry):
        x, y = other(p, 1)
        pl.semaphore_signal(barrier, inc=1, device_id=chip(x, y, pz, core), device_id_type=MESH)
        return carry

    lax.fori_loop(1, nx * ny, greet_plane, 0)
    twin = chip(px, py, pz, 1 - core)
    pl.semaphore_signal(barrier, inc=1, device_id=twin, device_id_type=MESH)

    lane8 = iota((8, 128), 1)
    sub8 = iota((8, 128), 0)

    local[0].wait()
    iys[0] = it[pl.ds(0, 96, stride=8), :]
    iys[1] = it[pl.ds(7, 96, stride=8), :]

    def pack_iterate(f, carry):
        low, high = carry
        start = pl.multiple_of(f * 32, 32)
        ixs[0, f] = it[pl.ds(start, 8), :]
        ixs[1, f] = it[pl.ds(start + 24, 8), :]
        for x in range(4):
            v = it[pl.ds(start + x * 8, 8), :]
            t = x * 32 + f
            low = jnp.where(lane8 == t, pltpu.roll(v, t, 1), low)
            high = jnp.where(lane8 == t, pltpu.roll(v, t + 1, 1), high)
        return low, high

    zero8 = jnp.zeros((8, 128), F32)
    low, high = lax.fori_loop(0, FIELDS, pack_iterate, (zero8, zero8), unroll=2)
    izs[0] = low
    izs[1] = high
    local[1].wait()
    for y in range(8):
        cbox[y + 2, 2:6] = cls[pl.ds(y, 4, stride=8), :] + 1

    acc[...] = it[...]
    for ref in (ga, gb, gc):
        ref[:, 0] = jnp.zeros((PER, 8, 128), F32)
        ref[:, 13] = jnp.zeros((PER, 8, 128), F32)
    for ref in (za, zc, zd):
        ref[0] = zero8
        ref[13] = zero8

    peers = nz - 1 + nx * ny - 1 + 1 + across_gx.astype(I32) + across_gy.astype(I32)
    pl.semaphore_wait(barrier, peers)

    cls_y = exchange("gy", cbox.at[2:4, 2:6], cbox.at[10:12, 2:6], cbox.at[8:10, 2:6], cbox.at[0:2, 2:6])
    it_y = exchange("gy", iys.at[0], iyr.at[1], iys.at[1], iyr.at[0])
    it_x = exchange("gx", ixs.at[0], ixr.at[1], ixs.at[1], ixr.at[0])
    it_z = exchange("gz", izs.at[0], izr.at[1], izs.at[1], izr.at[0])

    local[2].wait()

    def own_class(x):
        return cls[pl.ds(x * 8, 8), :]

    stiff_own = jnp.stack([lookup(own_class(x), stiffness) for x in range(4)])
    mass_own = jnp.stack([lookup(own_class(x), density) for x in range(4)])
    diag_own = 6.0 * stiff_own + mass_own - COUPLING * stiff_own

    it_x()
    it_z()

    def own_residual(col, carry):
        start = pl.multiple_of(col * 96, 96)
        u = it[pl.ds(start, 96), :].reshape(3, 4, 8, 128)
        lower = ixr[0, pl.ds(col * 3, 3)][:, None]
        upper = ixr[1, pl.ds(col * 3, 3)][:, None]
        near = jnp.concatenate([lower, u[:, :3]], 1) + jnp.concatenate([u[:, 1:], upper], 1)
        near = near + beside_x(u, 2)
        fill_low, fill_high = [], []
        for c in range(3):
            for x in range(4):
                t = x * 32 + col * 3 + c
                fill_low.append(pltpu.roll(izr[0], lax.rem(128 - t, 128), 1))
                fill_high.append(pltpu.roll(izr[1], 127 - t, 1))
        lane = iota(u.shape, 3)
        near = near + jnp.where(lane == 0, jnp.stack(fill_low).reshape(u.shape), pltpu.roll(u, 1, 3))
        near = near + jnp.where(lane == 127, jnp.stack(fill_high).reshape(u.shape), pltpu.roll(u, 127, 3))
        total = (u[0] + u[1] + u[2])[None]
        r = ld[pl.ds(start, 96), :].reshape(3, 4, 8, 128)
        r = r - diag_own[None] * u + stiff_own[None] * (near - COUPLING * total)
        res[pl.ds(start, 96), :] = r.reshape(96, 128)
        return carry

    lax.fori_loop(0, 8, own_residual, 0)

    def pack_rows(f, carry):
        for side in range(2):
            for layer in range(2):
                ys[side, f, layer * 4 : layer * 4 + 4] = res[pl.ds(f * 32 + side * 6 + layer, 4, stride=8), :]
        return carry

    lax.fori_loop(0, FIELDS, pack_rows, 0, unroll=2)
    res_y = []
    for ch in range(CHUNKS):
        fs = pl.ds(ch * PER, PER)
        res_y.append(exchange("gy", ys.at[0, fs], yr.at[1, fs], ys.at[1, fs], yr.at[0, fs]))

    local[3].wait()

    def prepare_basis(k, carry):
        hi, lo = halves(bas[pl.ds(k, 32, stride=96), :])
        at = pl.ds(pl.multiple_of(k * 128, 128), 128)
        bt[0:32, at] = hi
        bt[32:64, at] = lo
        bt[64:96, at] = hi
        bt[96:128, at] = jnp.zeros((32, 128), BF16)
        return carry

    lax.fori_loop(0, 96, prepare_basis, 0, unroll=2)

    def two(v):
        hi, lo = halves(v)
        return jnp.concatenate([hi, lo], 0)

    def coefficients(k, total):
        v = jnp.concatenate([res[pl.ds(k * 8 + i, 8, stride=96), :] for i in range(8)], 1)
        at = pl.ds(pl.multiple_of(k * 1024, 1024), 1024)
        return total + lax.dot_general(two(v), bt[0:64, at], NT, preferred_element_type=F32)

    coeff = lax.fori_loop(0, 12, coefficients, jnp.zeros((16, 64), F32))

    local[4].wait()

    def prepare_coarse(k, carry):
        at = pl.ds(pl.multiple_of(k * 512, 512), 512)
        hi, lo = halves(ci[:, at])
        c2[0:32, at] = hi
        c2[32:64, at] = lo
        return carry

    lax.fori_loop(0, ci.shape[1] // 512, prepare_coarse, 0)

    cls_y()
    cls_x = exchange("gx", cbox.at[:, 2:4], cbox.at[:, 6:8], cbox.at[:, 4:6], cbox.at[:, 0:2])
    cls_x()
    low = jnp.zeros((8, 128), I32)
    high = jnp.zeros((8, 128), I32)
    for y in range(12):
        mask = lane8 // 2 == y
        low = jnp.where(mask, pltpu.roll(cbox[y], 2 * y, 1), low)
        high = jnp.where(mask, pltpu.roll(cbox[y], 2 * y + 2, 1), high)
    czs[0] = low
    czs[1] = high
    cls_z = exchange("gz", czs.at[0], czr.at[1], czs.at[1], czr.at[0])
    cls_z()

    def factors(shifted):
        inside = shifted > 0
        stiff = lookup(shifted - 1, stiffness)
        mass = lookup(shifted - 1, density)
        weight = jnp.where(inside, DAMPING / jnp.where(inside, 6.0 * stiff + mass - COUPLING * stiff, 1.0), 0.0)
        return stiff, weight

    def box_factors(y, carry):
        stiff, weight = factors(cbox[y])
        sbox[y] = stiff
        wbox[y] = weight
        bbox[y] = stiff * weight
        base = lane8 % 2
        spread = jnp.zeros((8, 128), I32)
        for side in range(2):
            two_lanes = jnp.where(lane8 < 2, pltpu.roll(czr[side], 128 - 2 * y, 1), 0)
            pair = two_lanes + pltpu.roll(two_lanes, 2, 1)
            six = pair + pltpu.roll(pair, 4, 1) + pltpu.roll(pair, 8, 1)
            spread = spread + (six if side == 0 else pltpu.roll(six, 12, 1))
        stiff, weight = factors(spread)
        zw[y] = weight
        zb[y] = stiff * weight
        return carry

    lax.fori_loop(0, 12, box_factors, 0)

    it_y()
    parts, columns = [], []
    for side in range(2):
        row = cls[pl.ds(side * 7, 4, stride=8), :]
        stiff = lookup(jnp.concatenate([row, row], 0), stiffness)
        v = (iyr[side].reshape(12, 8, 128) * stiff[None]).reshape(96, 128)
        vy[side] = v
        res[pl.ds(side * 7, 96, stride=8), :] = res[pl.ds(side * 7, 96, stride=8), :] + v
    for side in range(2):
        for cx in range(12):
            k = cx * 8 + side * 7
            parts.append(vy[side, pl.ds(cx, 8, stride=12), :])
            columns.append(bt[0:64, k * 128 : k * 128 + 128])
    coeff = coeff + lax.dot_general(
        two(jnp.concatenate(parts, 1)), jnp.concatenate(columns, 1), NT, preferred_element_type=F32
    )

    def quarters(v):
        v = v[0:8] + v[8:16]
        v = v[:, 0:32] + v[:, 32:64]
        return jnp.concatenate([v, jnp.zeros((8, 96), F32)], 1)

    mine = quarters(coeff)
    packed = zero8
    for q in range(4):
        v = pltpu.roll(mine, 32 * q, 1) if q else mine
        v = pltpu.roll(v, 8 - q, 0) if q else v
        packed = jnp.where(lane8 // 32 == q, v, packed)
    g1[pz, 0:1] = packed[0:1]
    g1[pz, 1:2] = packed[4:5]
    line = count[0]
    count[0] += nz
    plane = count[0]
    count[0] += nx * ny
    twins = count[0]
    count[0] += nx * ny

    def along_line(k):
        to = chip(px, py, lax.rem(pz + k, nz), core)
        return pltpu.make_async_remote_copy(g1.at[pz], g1.at[pz], ss.at[line + k], rs.at[line + k], to, MESH)

    def start_line(k, carry):
        along_line(k).start()
        return carry

    lax.fori_loop(1, nz, start_line, 0)

    def own_rows(f, carry):
        for y in range(8):
            box[f, y + 2, 2:6] = res[pl.ds(f * 32 + y, 4, stride=8), :]
        return carry

    lax.fori_loop(0, FIELDS, own_rows, 0, unroll=2)
    own_x = exchange("gx", box.at[:, 2:10, 2:4], box.at[:, 2:10, 6:8], box.at[:, 2:10, 4:6], box.at[:, 2:10, 0:2])

    res_x, res_z = {}, {}

    def rows_arrive(ch):
        res_y[ch]()
        fs = pl.ds(ch * PER, PER)
        _, has_lower, _, has_upper = steps["gy"]

        @pl.when(has_lower)
        def _():
            for f in range(ch * PER, ch * PER + PER):
                v = yr[0, f]
                box[f, 0, 2:6] = v[0:4]
                box[f, 1, 2:6] = v[4:8] + sbox[1, 2:6] * iys[0, f * 4 : f * 4 + 4]

        @pl.when(has_upper)
        def _():
            for f in range(ch * PER, ch * PER + PER):
                v = yr[1, f]
                box[f, 10, 2:6] = v[0:4] + sbox[10, 2:6] * iys[1, f * 4 : f * 4 + 4]
                box[f, 11, 2:6] = v[4:8]

        first = exchange("gx", box.at[fs, 0:2, 2:4], box.at[fs, 0:2, 6:8], box.at[fs, 0:2, 4:6], box.at[fs, 0:2, 0:2])
        second = exchange(
            "gx", box.at[fs, 10:12, 2:4], box.at[fs, 10:12, 6:8], box.at[fs, 10:12, 4:6], box.at[fs, 10:12, 0:2]
        )
        res_x[ch] = (first, second)

    def planes_arrive(ch):
        if ch == 0:
            own_x()
        for arrived in res_x[ch]:
            arrived()
        lane = iota((12, 8, 128), 2)
        low = jnp.zeros((12, 8, 128), F32)
        high = jnp.zeros((12, 8, 128), F32)
        for i in range(PER):
            v = box[ch * PER + i]
            mask = lane // 2 == i
            low = jnp.where(mask, pltpu.roll(v, 2 * i, 2) if i else v, low)
            high = jnp.where(mask, pltpu.roll(v, 2 * i + 2, 2), high)
        for side, v in enumerate((low, high)):
            first, second = zero8, zero8
            for y in range(12):
                t = (y % 10) * 12
                w = pltpu.roll(v[y], t, 1) if t else v[y]
                if y < 10:
                    first = first + w
                else:
                    second = second + w
            zs[ch, side, 0] = first
            zs[ch, side, 1] = second
        res_z[ch] = exchange("gz", zs.at[ch, 0], zr.at[ch, 1], zs.at[ch, 1], zr.at[ch, 0])

    def sweep(src, zsrc, dst, zdst, y):
        e, z = src[:, y], zsrc[y]
        lane, lane6 = lane8, iota((PER, 8, 128), 2)
        near = src[:, y - 1] + src[:, y + 1] + beside_x(e, 1)
        fill_low = jnp.stack([pltpu.roll(z, 127 - 2 * i, 1) for i in range(PER)])
        fill_high = jnp.stack([pltpu.roll(z, 115 - 2 * i, 1) for i in range(PER)])
        near = near + jnp.where(lane6 == 0, fill_low, pltpu.roll(e, 1, 2))
        near = near + jnp.where(lane6 == 127, fill_high, pltpu.roll(e, 127, 2))
        totals = jnp.stack([e[0] + e[1] + e[2]] * 3 + [e[3] + e[4] + e[5]] * 3)
        dst_value = ga[:, y] + (1.0 - DAMPING) * e + bbox[y - 1][None] * (near - COUPLING * totals)
        if zdst is not None:
            dst[:, y] = dst_value
            push = jnp.zeros((8, 128), F32)
            for i in range(PER):
                push = jnp.where(lane == 2 * i + 1, pltpu.roll(e[i], 2 * i + 1, 1), push)
                push = jnp.where(lane == 12 + 2 * i, pltpu.roll(e[i], 13 + 2 * i, 1), push)
            back, ahead = pltpu.roll(z, 1, 1), pltpu.roll(z, 127, 1)
            znear = zsrc[y - 1] + zsrc[y + 1] + beside_x(z, 0) + push + jnp.where(lane % 2 == 0, ahead, back)
            two_on, four_on = pltpu.roll(z, 126, 1), pltpu.roll(z, 124, 1)
            two_back, four_back = pltpu.roll(z, 2, 1), pltpu.roll(z, 4, 1)
            comp = (lane // 2) % 3
            rest = jnp.where(
                comp == 0, two_on + four_on, jnp.where(comp == 1, two_on + two_back, two_back + four_back)
            )
            zdst[y] = za[y] + (1.0 - DAMPING) * z + zb[y - 1] * (znear - COUPLING * (z + rest))
        return dst_value

    def sweeps(ch):
        res_z[ch]()

        def start(y, carry):
            ga[:, y + 1] = box[pl.ds(ch * PER, PER), y] * wbox[y][None]
            return carry

        lax.fori_loop(0, 12, start, 0)
        for y in range(12):
            t = (y % 10) * 12
            low, high = zr[ch, 0, y // 10], zr[ch, 1, y // 10]
            low = pltpu.roll(low, 128 - t, 1) if t else low
            high = pltpu.roll(high, (140 - t) % 128, 1) if t != 12 else high
            z = jnp.where(lane8 < 12, low, jnp.where(lane8 < 24, high, 0.0))
            za[y + 1] = z * zw[y]

        def first(y, carry):
            sweep(ga, za, gb, zc, y)
            return carry

        lax.fori_loop(1, 13, first, 0)

        def second(y, carry):
            sweep(gb, zc, gc, zd, y)
            return carry

        lax.fori_loop(2, 12, second, 0)

        def third(y, carry):
            v = sweep(gc, zd, None, None, y)
            for i in range(PER):
                at = pl.ds((ch * PER + i) * 32 + y - 3, 4, stride=8)
                acc[at, :] = acc[at, :] + v[i, 2:6]
            return carry

        lax.fori_loop(3, 11, third, 0)

    def block(x, y, c):
        return (y * 2 + c) * nx + x

    def along_plane(p):
        x, y = other(p, 1)
        b = block(px, py, core)
        return pltpu.make_async_remote_copy(
            g2.at[b], g2.at[b], ss.at[plane + p], rs.at[plane + p], chip(x, y, pz, core), MESH
        )

    def to_twin(p):
        x, y = other(p, -1)
        b = block(x, y, core)
        return pltpu.make_async_remote_copy(g2.at[b], g2.at[b], ss.at[twins + p], rs.at[twins + p], twin, MESH)

    def line_arrives():
        def arrive(k, carry):
            along_line(k).wait_recv()
            return carry

        lax.fori_loop(1, nz, arrive, 0)
        groups = nz // 4
        rows = g1[...]
        upper = jnp.broadcast_to(rows[:, 0:1], (nz, 8, 128))
        lower = jnp.broadcast_to(rows[:, 1:2], (nz, 8, 128))
        both = jnp.where(iota((nz, 8, 128), 1) < 4, upper, lower).reshape(groups, 4, 8, 128)
        lane, sub = iota((groups, 8, 128), 2) // 32, iota((groups, 8, 128), 1) % 4
        spread = jnp.zeros((groups, 8, 128), F32)
        for zz in range(4):
            for q in range(4):
                t = 32 * ((zz - q) % 4)
                v = both[:, zz]
                v = pltpu.roll(v, t, 2) if t else v
                spread = jnp.where((lane == zz) & (sub == q), v, spread)
        b = block(px, py, core)
        g2[b] = jnp.concatenate([spread[i] for i in range(groups)], 1)

        def start(p, carry):
            along_plane(p).start()
            return carry

        lax.fori_loop(1, nx * ny, start, 0)
        to_twin(0).start()

    width = nz * 32

    def times_block(b, total):
        at = pl.ds(pl.multiple_of(b * width, width), width)
        return total + lax.dot_general(two(g2[b]), c2[:, at], NT, preferred_element_type=F32)

    def plane_arrives():
        def arrive(p, total):
            along_plane(p).wait_recv()
            to_twin(p).start()
            x, y = other(p, -1)
            return times_block(block(x, y, core), total)

        return lax.fori_loop(1, nx * ny, arrive, times_block(block(px, py, core), jnp.zeros((16, 64), F32)))

    def twins_arrive(total):
        def arrive(p, total):
            to_twin(p).wait_recv()
            x, y = other(p, -1)
            return times_block(block(x, y, 1 - core), total)

        total = lax.fori_loop(0, nx * ny, arrive, total)
        solved = quarters(total)
        hi = solved.astype(BF16).astype(F32)
        lo = solved - hi
        factor = hi + pltpu.roll(hi, 32, 1) + pltpu.roll(lo, 64, 1)
        factor = factor.astype(BF16)

        def correct(k, carry):
            at = pl.ds(pl.multiple_of(k * 1024, 1024), 1024)
            v = jnp.dot(factor, bt[:, at], preferred_element_type=F32)
            for i in range(8):
                rows = pl.ds(k * 8 + i, 8, stride=96)
                acc[rows, :] = acc[rows, :] + v[:, i * 128 : i * 128 + 128]
            return carry

        lax.fori_loop(0, 12, correct, 0)

    rows_arrive(0)
    line_arrives()
    rows_arrive(1)
    planes_arrive(0)
    rows_arrive(2)
    planes_arrive(1)
    sweeps(0)
    total = plane_arrives()
    rows_arrive(3)
    planes_arrive(2)
    sweeps(1)
    planes_arrive(3)
    twins_arrive(total)
    sweeps(2)
    sweeps(3)
    done = pltpu.make_async_copy(acc, out, ls.at[5])
    done.start()

    for sent in pending:
        sent()

    def all_sent(k, carry):
        along_line(k).wait_send()
        return carry

    lax.fori_loop(1, nz, all_sent, 0)

    def all_sent_plane(p, carry):
        along_plane(p).wait_send()
        to_twin(p).wait_send()
        return carry

    to_twin(0).wait_send()
    lax.fori_loop(1, nx * ny, all_sent_plane, 0)
    done.wait()


def solution(mesh):
    ny, nx, nz = mesh.shape["gx"] // 2, mesh.shape["gy"] // 2, mesh.shape["gz"] * 2
    nc = 2 * ny * nx * nz * 32

    def step(loads, iterate, classes, stiffness, density, basis, coarse_inverse):
        v = pltpu.VMEM
        scratch = [
            v((768, 128), F32), v((768, 128), F32), v((768, 128), F32), v((32, 128), I32), v((3072, 128), F32),
            v((32, nc), F32), v((768, 128), F32),
            v((2, 96, 128), F32), v((2, 96, 128), F32), v((2, FIELDS, 8, 128), F32), v((2, FIELDS, 8, 128), F32),
            v((2, 8, 128), F32), v((2, 8, 128), F32),
            v((12, 8, 128), I32), v((2, 8, 128), I32), v((2, 8, 128), I32),
            v((FIELDS, 12, 8, 128), F32), v((2, FIELDS, 8, 128), F32), v((2, FIELDS, 8, 128), F32),
            v((CHUNKS, 2, 2, 8, 128), F32), v((CHUNKS, 2, 2, 8, 128), F32),
            v((128, 12288), BF16), v((64, nc), BF16),
            v((nz, 2, 128), F32), v((2 * ny * nx, 8, nz * 32), F32),
            v((12, 8, 128), F32), v((12, 8, 128), F32), v((12, 8, 128), F32), v((12, 8, 128), F32),
            v((12, 8, 128), F32),
            v((PER, 14, 8, 128), F32), v((PER, 14, 8, 128), F32), v((PER, 14, 8, 128), F32),
            v((14, 8, 128), F32), v((14, 8, 128), F32), v((14, 8, 128), F32),
            v((2, 96, 128), F32),
            pltpu.SemaphoreType.DMA((128,)), pltpu.SemaphoreType.DMA((128,)), pltpu.SemaphoreType.DMA((6,)),
        ]
        hbm, smem = pl.BlockSpec(memory_space=pl.ANY), pl.BlockSpec(memory_space=pltpu.SMEM)
        result = pl.pallas_call(
            functools.partial(kernel, ny, nx, nz),
            out_shape=jax.ShapeDtypeStruct((768, 128), F32),
            in_specs=[hbm, hbm, hbm, smem, smem, hbm, hbm],
            out_specs=hbm,
            scratch_shapes=scratch,
            compiler_params=pltpu.CompilerParams(
                collective_id=0, has_side_effects=True, vmem_limit_bytes=48 * 1024 * 1024
            ),
            name="schwarz",
        )(
            loads.reshape(768, 128), iterate.reshape(768, 128), classes.reshape(32, 128), stiffness, density,
            basis.reshape(3072, 128), coarse_inverse,
        )
        return result.reshape(iterate.shape)

    field = P(None, None, "gx", "gy", "gz")
    return jax.shard_map(
        step,
        mesh=mesh,
        in_specs=(field, field, P("gx", "gy", "gz"), P(), P(), field, P(("gx", "gy", "gz"), None)),
        out_specs=field,
        check_vma=False,
    )
```

time: 313 us -> 93.3 us (0.30)
  the two profiles are of different devices: /device:TPU:32 before, /device:TPU:1 now
where the time goes in v1:
time: 93.3 us; the launch traced here: 92 us
  Pallas kernels  84.2 us (90%)
  local copies, waits for them, and re-layouts  7.76 us (8%)
    pallas_call x1, Pallas kernels, step(): pl.pallas_call(functools.partial(kernel, ny, nx, nz), out_shape=jax.Shape...  84.2 us
    unnamed x15, local copies, waits for them, and re-layouts  7.76 us

profile of v1, /device:TPU:1, one launch (start us, length us, event | category | flops | bytes accessed | tf_op | source)
XLA Modules:
  0.0 92.0 jit_solution(13970577127098613771)
XLA Ops:
  0.0 0.0 copy-start
  0.0 1.6 %copy-done = f32[32,16384]{1,0:T(8,128)S(1)} copy-done((f32[32,16384]{1,0:T(8,128)S(1)}, f32[32,16384]{1,0:T(8,128)}, u32[]{:S(2)}) %copy-start) | copy-done | bytes 2097176
  1.6 0.0 copy-start.1
  1.6 1.4 %copy-done.1 = f32[32,3,4,8,128]{4,3,2,1,0:T(8,128)S(1)} copy-done((f32[32,3,4,8,128]{4,3,2,1,0:T(8,128)S(1)}, f32[32,3,4,8,128]{4,3,2,1,0:T(8,128)}, u32[]{:S(2)}) %copy-start.1) | copy-done | bytes 1572888
  3.0 0.0 copy-start.2
  3.0 1.0 %copy-done.2 = f32[8,3,4,8,128]{4,3,2,1,0:T(8,128)S(1)} copy-done((f32[8,3,4,8,128]{4,3,2,1,0:T(8,128)S(1)}, f32[8,3,4,8,128]{4,3,2,1,0:T(8,128)}, u32[]{:S(2)}) %copy-start.2) | copy-done | bytes 393240
  4.0 0.0 copy-start.3
  4.0 1.0 %copy-done.3 = f32[8,3,4,8,128]{4,3,2,1,0:T(8,128)S(1)} copy-done((f32[8,3,4,8,128]{4,3,2,1,0:T(8,128)S(1)}, f32[8,3,4,8,128]{4,3,2,1,0:T(8,128)}, u32[]{:S(2)}) %copy-start.3) | copy-done | bytes 393240
  5.0 0.0 copy-start.4
  5.0 0.7 copy-done.4
  5.7 0.0 copy-start.5
  5.7 0.7 copy-done.5
  6.4 0.0 copy-start.6
  6.4 0.7 copy-done.6
  7.0 84.2 %schwarz.1 = f32[768,128]{1,0:T(8,128)S(1)} custom-call(f32[768,128]{1,0:T(8,128)S(1)} %bitcast.7, f32[768,128]{1,0:T(8,128)S(1)} %bitcast.8, s32[32,128]{1,0:T(8,128)S(1)} %bitcast.9, f32[8]{0:T(128)S(1)} %copy-done.5, f32[8]{0:T(128)S(1)} %copy-done.6, f32[3072,128]{1,0:T(8,128)S(1)} %bitcast.5, f32[32,16384]{1,0:T(8,128)S(1)} %copy-done), custom_call_target="tpu_custom_call" | custom-call | tf_op jit(solution)/shard_map/schwarz/pallas_call | solution.py:597
  91.2 0.7 copy.9
Async XLA Ops:
  0.0 1.6 %copy-start = (f32[32,16384]{1,0:T(8,128)S(1)}, f32[32,16384]{1,0:T(8,128)}, u32[]{:S(2)}) copy-start(f32[32,16384]{1,0:T(8,128)} %cinv.1) | copy-start | bytes 6291460
  1.6 1.4 %copy-start.1 = (f32[32,3,4,8,128]{4,3,2,1,0:T(8,128)S(1)}, f32[32,3,4,8,128]{4,3,2,1,0:T(8,128)}, u32[]{:S(2)}) copy-start(f32[32,3,4,8,128]{4,3,2,1,0:T(8,128)} %param.12) | copy-start | bytes 4718596
  3.0 1.0 %copy-start.2 = (f32[8,3,4,8,128]{4,3,2,1,0:T(8,128)S(1)}, f32[8,3,4,8,128]{4,3,2,1,0:T(8,128)}, u32[]{:S(2)}) copy-start(f32[8,3,4,8,128]{4,3,2,1,0:T(8,128)} %param.7) | copy-start | bytes 1179652
  4.0 1.0 %copy-start.3 = (f32[8,3,4,8,128]{4,3,2,1,0:T(8,128)S(1)}, f32[8,3,4,8,128]{4,3,2,1,0:T(8,128)}, u32[]{:S(2)}) copy-start(f32[8,3,4,8,128]{4,3,2,1,0:T(8,128)} %param.8) | copy-start | bytes 1179652
  5.0 0.7 copy-start.4
  5.7 0.7 copy-start.5
  6.4 0.7 copy-start.6

commit v2 on v1

--- a/solution.py
+++ b/solution.py
@@ -37,9 +37,9 @@
 
 
 def kernel(
-    ny, nx, nz, loads, iterate, classes, stiffness, density, basis, cinv, out,
-    it, ld, acc, cls, bas, ci, res, iys, iyr, ixs, ixr, izs, izr, cbox, czs, czr, box, ys, yr,
-    zs, zr, bt, c2, g1, g2, sbox, wbox, bbox, zw, zb, ga, gb, gc, za, zc, zd, vy,
+    ny, nx, nz, loads, iterate, classes, stiffness_in, density_in, basis, cinv, acc,
+    it, ld, cls, stiffness, density, bas, ci, res, iys, iyr, ixs, ixr, izs, izr, cbox, czs, czr, box, ys, yr,
+    zs, zr, bh, bl, bf, c2, g1, g2, sbox, wbox, bbox, zw, zb, ga, gb, gc, za, zc, zd, vy,
     ss, rs, ls,
 ):
     gx, gy, gz = lax.axis_index("gx"), lax.axis_index("gy"), lax.axis_index("gz")
@@ -79,7 +79,12 @@
 
     local = [
         pltpu.make_async_copy(a, b, ls.at[i])
-        for i, (a, b) in enumerate(((iterate, it), (classes, cls), (loads, ld), (basis, bas), (cinv, ci)))
+        for i, (a, b) in enumerate(
+            (
+                (iterate, it), (classes, cls), (loads, ld), (basis, bas), (cinv, ci),
+                (stiffness_in, stiffness), (density_in, density),
+            )
+        )
     ]
     for copy in local:
         copy.start()
@@ -156,6 +161,8 @@
     it_x = exchange("gx", ixs.at[0], ixr.at[1], ixs.at[1], ixr.at[0])
     it_z = exchange("gz", izs.at[0], izr.at[1], izs.at[1], izr.at[0])
 
+    local[5].wait()
+    local[6].wait()
     local[2].wait()
 
     def own_class(x):
@@ -199,34 +206,55 @@
         return carry
 
     lax.fori_loop(0, FIELDS, pack_rows, 0, unroll=2)
-    res_y = []
-    for ch in range(CHUNKS):
+    res_y = {}
+
+    def send_rows(ch):
         fs = pl.ds(ch * PER, PER)
-        res_y.append(exchange("gy", ys.at[0, fs], yr.at[1, fs], ys.at[1, fs], yr.at[0, fs]))
+        res_y[ch] = exchange("gy", ys.at[0, fs], yr.at[1, fs], ys.at[1, fs], yr.at[0, fs])
+
+    send_rows(0)
+    send_rows(1)
 
     local[3].wait()
 
     def prepare_basis(k, carry):
-        hi, lo = halves(bas[pl.ds(k, 32, stride=96), :])
-        at = pl.ds(pl.multiple_of(k * 128, 128), 128)
-        bt[0:32, at] = hi
-        bt[32:64, at] = lo
-        bt[64:96, at] = hi
-        bt[96:128, at] = jnp.zeros((32, 128), BF16)
-        return carry
-
-    lax.fori_loop(0, 96, prepare_basis, 0, unroll=2)
+        for cx in range(12):
+            v = jnp.concatenate([bas[pl.ds((k * 4 + i) * 96 + cx * 8, 8), :] for i in range(4)], 0)
+            rows = pl.ds(pl.multiple_of(k * 32, 32), 32)
+            bh[rows, cx * 128 : cx * 128 + 128], bl[rows, cx * 128 : cx * 128 + 128] = halves(v)
+        return carry
+
+    lax.fori_loop(0, 8, prepare_basis, 0)
+    for side in range(2):
+        for cx in range(12):
+            at = slice((side * 12 + cx) * 128, (side * 12 + cx) * 128 + 128)
+            bf[0:32, at], bf[32:64, at] = halves(bas[pl.ds(cx * 8 + side * 7, 32, stride=96), :])
 
     def two(v):
         hi, lo = halves(v)
         return jnp.concatenate([hi, lo], 0)
 
     def coefficients(k, total):
-        v = jnp.concatenate([res[pl.ds(k * 8 + i, 8, stride=96), :] for i in range(8)], 1)
-        at = pl.ds(pl.multiple_of(k * 1024, 1024), 1024)
-        return total + lax.dot_general(two(v), bt[0:64, at], NT, preferred_element_type=F32)
-
-    coeff = lax.fori_loop(0, 12, coefficients, jnp.zeros((16, 64), F32))
+        v = jnp.concatenate(
+            [
+                jnp.concatenate([res[pl.ds(col * 96 + (k * 2 + i) * 8, 8), :] for col in range(8)], 0)
+                for i in range(2)
+            ],
+            1,
+        )
+        at = pl.ds(pl.multiple_of(k * 256, 256), 256)
+        hi, lo = halves(v)
+        total = total + lax.dot_general(hi, bh[:, at], NT, preferred_element_type=F32)
+        total = total + lax.dot_general(lo, bh[:, at], NT, preferred_element_type=F32)
+        return total + lax.dot_general(hi, bl[:, at], NT, preferred_element_type=F32)
+
+    pairs = lax.fori_loop(0, 6, coefficients, jnp.zeros((64, 256), F32), unroll=6)
+    equal = iota((64, 256), 0) % 8 == iota((64, 256), 1) % 8
+    sums = jnp.sum(jnp.where(equal, pairs, 0.0).reshape(8, 8, 256), 1)
+    fold = (iota((256, 128), 0) // 8 == iota((256, 128), 1)).astype(BF16)
+    folded = jnp.dot(two(sums), fold, preferred_element_type=F32)
+    coeff = folded[0:8] + folded[8:16]
+    unfold = (iota((128, 256), 0) == iota((128, 256), 1) // 8).astype(BF16)
 
     local[4].wait()
 
@@ -237,7 +265,7 @@
         c2[32:64, at] = lo
         return carry
 
-    lax.fori_loop(0, ci.shape[1] // 512, prepare_coarse, 0)
+    lax.fori_loop(0, ci.shape[1] // 512, prepare_coarse, 0, unroll=2)
 
     cls_y()
     cls_x = exchange("gx", cbox.at[:, 2:4], cbox.at[:, 6:8], cbox.at[:, 4:6], cbox.at[:, 0:2])
@@ -253,6 +281,14 @@
     cls_z = exchange("gz", czs.at[0], czr.at[1], czs.at[1], czr.at[0])
     cls_z()
 
+    def z_lanes(low, high, t, width):
+        odd = lane8 % 2 == 1
+        low, high = pltpu.roll(low, (128 - t) % 128, 1), pltpu.roll(high, (128 - t) % 128, 1)
+        inner = jnp.where(odd, low, high)
+        outer = jnp.where(odd, pltpu.roll(low, 1, 1), pltpu.roll(high, 127, 1))
+        zero = jnp.zeros_like(inner)
+        return jnp.where(lane8 < width, inner, zero) + pltpu.roll(jnp.where(lane8 < width, outer, zero), 64, 1)
+
     def factors(shifted):
         inside = shifted > 0
         stiff = lookup(shifted - 1, stiffness)
@@ -265,43 +301,33 @@
         sbox[y] = stiff
         wbox[y] = weight
         bbox[y] = stiff * weight
-        base = lane8 % 2
-        spread = jnp.zeros((8, 128), I32)
-        for side in range(2):
-            two_lanes = jnp.where(lane8 < 2, pltpu.roll(czr[side], 128 - 2 * y, 1), 0)
-            pair = two_lanes + pltpu.roll(two_lanes, 2, 1)
-            six = pair + pltpu.roll(pair, 4, 1) + pltpu.roll(pair, 8, 1)
-            spread = spread + (six if side == 0 else pltpu.roll(six, 12, 1))
+        spread = z_lanes(czr[0], czr[1], 2 * y, 2)
+        pair = spread + pltpu.roll(spread, 2, 1)
+        spread = pair + pltpu.roll(pair, 4, 1) + pltpu.roll(pair, 8, 1)
         stiff, weight = factors(spread)
         zw[y] = weight
         zb[y] = stiff * weight
         return carry
 
-    lax.fori_loop(0, 12, box_factors, 0)
+    lax.fori_loop(0, 12, box_factors, 0, unroll=6)
 
     it_y()
-    parts, columns = [], []
+    parts = []
     for side in range(2):
         row = cls[pl.ds(side * 7, 4, stride=8), :]
         stiff = lookup(jnp.concatenate([row, row], 0), stiffness)
-        v = (iyr[side].reshape(12, 8, 128) * stiff[None]).reshape(96, 128)
-        vy[side] = v
-        res[pl.ds(side * 7, 96, stride=8), :] = res[pl.ds(side * 7, 96, stride=8), :] + v
+        vy[side] = (iyr[side].reshape(12, 8, 128) * stiff[None]).reshape(96, 128)
     for side in range(2):
         for cx in range(12):
-            k = cx * 8 + side * 7
             parts.append(vy[side, pl.ds(cx, 8, stride=12), :])
-            columns.append(bt[0:64, k * 128 : k * 128 + 128])
-    coeff = coeff + lax.dot_general(
-        two(jnp.concatenate(parts, 1)), jnp.concatenate(columns, 1), NT, preferred_element_type=F32
-    )
+    faces = lax.dot_general(two(jnp.concatenate(parts, 1)), bf[...], NT, preferred_element_type=F32)
 
     def quarters(v):
         v = v[0:8] + v[8:16]
         v = v[:, 0:32] + v[:, 32:64]
         return jnp.concatenate([v, jnp.zeros((8, 96), F32)], 1)
 
-    mine = quarters(coeff)
+    mine = coeff + quarters(faces)
     packed = zero8
     for q in range(4):
         v = pltpu.roll(mine, 32 * q, 1) if q else mine
@@ -325,6 +351,11 @@
         return carry
 
     lax.fori_loop(1, nz, start_line, 0)
+    send_rows(2)
+    send_rows(3)
+    for side in range(2):
+        at = pl.ds(side * 7, 96, stride=8)
+        res[at, :] = res[at, :] + vy[side]
 
     def own_rows(f, carry):
         for y in range(8):
@@ -391,23 +422,20 @@
         e, z = src[:, y], zsrc[y]
         lane, lane6 = lane8, iota((PER, 8, 128), 2)
         near = src[:, y - 1] + src[:, y + 1] + beside_x(e, 1)
-        fill_low = jnp.stack([pltpu.roll(z, 127 - 2 * i, 1) for i in range(PER)])
-        fill_high = jnp.stack([pltpu.roll(z, 115 - 2 * i, 1) for i in range(PER)])
-        near = near + jnp.where(lane6 == 0, fill_low, pltpu.roll(e, 1, 2))
-        near = near + jnp.where(lane6 == 127, fill_high, pltpu.roll(e, 127, 2))
+        fill = jnp.stack([pltpu.roll(z, 127 - 2 * i, 1) for i in range(PER)])
+        near = near + jnp.where(lane6 == 0, fill, pltpu.roll(e, 1, 2))
+        near = near + jnp.where(lane6 == 127, fill, pltpu.roll(e, 127, 2))
         totals = jnp.stack([e[0] + e[1] + e[2]] * 3 + [e[3] + e[4] + e[5]] * 3)
         dst_value = ga[:, y] + (1.0 - DAMPING) * e + bbox[y - 1][None] * (near - COUPLING * totals)
         if zdst is not None:
             dst[:, y] = dst_value
             push = jnp.zeros((8, 128), F32)
             for i in range(PER):
-                push = jnp.where(lane == 2 * i + 1, pltpu.roll(e[i], 2 * i + 1, 1), push)
-                push = jnp.where(lane == 12 + 2 * i, pltpu.roll(e[i], 13 + 2 * i, 1), push)
-            back, ahead = pltpu.roll(z, 1, 1), pltpu.roll(z, 127, 1)
-            znear = zsrc[y - 1] + zsrc[y + 1] + beside_x(z, 0) + push + jnp.where(lane % 2 == 0, ahead, back)
+                push = jnp.where(lane // 2 == i, pltpu.roll(e[i], 2 * i + 1, 1), push)
+            znear = zsrc[y - 1] + zsrc[y + 1] + beside_x(z, 0) + push + pltpu.roll(z, 64, 1)
             two_on, four_on = pltpu.roll(z, 126, 1), pltpu.roll(z, 124, 1)
             two_back, four_back = pltpu.roll(z, 2, 1), pltpu.roll(z, 4, 1)
-            comp = (lane // 2) % 3
+            comp = ((lane % 64) // 2) % 3
             rest = jnp.where(
                 comp == 0, two_on + four_on, jnp.where(comp == 1, two_on + two_back, two_back + four_back)
             )
@@ -424,23 +452,20 @@
         lax.fori_loop(0, 12, start, 0)
         for y in range(12):
             t = (y % 10) * 12
-            low, high = zr[ch, 0, y // 10], zr[ch, 1, y // 10]
-            low = pltpu.roll(low, 128 - t, 1) if t else low
-            high = pltpu.roll(high, (140 - t) % 128, 1) if t != 12 else high
-            z = jnp.where(lane8 < 12, low, jnp.where(lane8 < 24, high, 0.0))
+            z = z_lanes(zr[ch, 0, y // 10], zr[ch, 1, y // 10], t, 2 * PER)
             za[y + 1] = z * zw[y]
 
         def first(y, carry):
             sweep(ga, za, gb, zc, y)
             return carry
 
-        lax.fori_loop(1, 13, first, 0)
+        lax.fori_loop(1, 13, first, 0, unroll=12)
 
         def second(y, carry):
             sweep(gb, zc, gc, zd, y)
             return carry
 
-        lax.fori_loop(2, 12, second, 0)
+        lax.fori_loop(2, 12, second, 0, unroll=10)
 
         def third(y, carry):
             v = sweep(gc, zd, None, None, y)
@@ -449,7 +474,7 @@
                 acc[at, :] = acc[at, :] + v[i, 2:6]
             return carry
 
-        lax.fori_loop(3, 11, third, 0)
+        lax.fori_loop(3, 11, third, 0, unroll=8)
 
     def block(x, y, c):
         return (y * 2 + c) * nx + x
@@ -518,38 +543,39 @@
 
         total = lax.fori_loop(0, nx * ny, arrive, total)
         solved = quarters(total)
-        hi = solved.astype(BF16).astype(F32)
-        lo = solved - hi
-        factor = hi + pltpu.roll(hi, 32, 1) + pltpu.roll(lo, 64, 1)
-        factor = factor.astype(BF16)
+        spread = jnp.dot(two(solved), unfold, preferred_element_type=F32)
+        spread = spread[0:8] + spread[8:16]
+        rows = jnp.broadcast_to(spread[:, None], (8, 8, 256)).reshape(64, 256)
+        hi, lo = halves(jnp.where(equal, rows, 0.0))
 
         def correct(k, carry):
-            at = pl.ds(pl.multiple_of(k * 1024, 1024), 1024)
-            v = jnp.dot(factor, bt[:, at], preferred_element_type=F32)
-            for i in range(8):
-                rows = pl.ds(k * 8 + i, 8, stride=96)
-                acc[rows, :] = acc[rows, :] + v[:, i * 128 : i * 128 + 128]
+            at = pl.ds(pl.multiple_of(k * 256, 256), 256)
+            v = jnp.dot(hi, bh[:, at], preferred_element_type=F32)
+            v = v + jnp.dot(lo, bh[:, at], preferred_element_type=F32)
+            v = v + jnp.dot(hi, bl[:, at], preferred_element_type=F32)
+            for col in range(8):
+                for i in range(2):
+                    rows = pl.ds(pl.multiple_of(col * 96 + (k * 2 + i) * 8, 8), 8)
+                    acc[rows, :] = acc[rows, :] + v[col * 8 : col * 8 + 8, i * 128 : i * 128 + 128]
             return carry
 
-        lax.fori_loop(0, 12, correct, 0)
+        lax.fori_loop(0, 6, correct, 0, unroll=6)
 
     rows_arrive(0)
-    line_arrives()
     rows_arrive(1)
     planes_arrive(0)
-    rows_arrive(2)
+    line_arrives()
     planes_arrive(1)
     sweeps(0)
+    rows_arrive(2)
+    sweeps(1)
+    planes_arrive(2)
+    rows_arrive(3)
     total = plane_arrives()
-    rows_arrive(3)
-    planes_arrive(2)
-    sweeps(1)
-    planes_arrive(3)
     twins_arrive(total)
     sweeps(2)
+    planes_arrive(3)
     sweeps(3)
-    done = pltpu.make_async_copy(acc, out, ls.at[5])
-    done.start()
 
     for sent in pending:
         sent()
@@ -567,7 +593,6 @@
 
     to_twin(0).wait_send()
     lax.fori_loop(1, nx * ny, all_sent_plane, 0)
-    done.wait()
 
 
 def solution(mesh):
@@ -577,31 +602,32 @@
     def step(loads, iterate, classes, stiffness, density, basis, coarse_inverse):
         v = pltpu.VMEM
         scratch = [
-            v((768, 128), F32), v((768, 128), F32), v((768, 128), F32), v((32, 128), I32), v((3072, 128), F32),
+            v((768, 128), F32), v((768, 128), F32), v((32, 128), I32),
+            pltpu.SMEM((8,), F32), pltpu.SMEM((8,), F32), v((3072, 128), F32),
             v((32, nc), F32), v((768, 128), F32),
             v((2, 96, 128), F32), v((2, 96, 128), F32), v((2, FIELDS, 8, 128), F32), v((2, FIELDS, 8, 128), F32),
             v((2, 8, 128), F32), v((2, 8, 128), F32),
             v((12, 8, 128), I32), v((2, 8, 128), I32), v((2, 8, 128), I32),
             v((FIELDS, 12, 8, 128), F32), v((2, FIELDS, 8, 128), F32), v((2, FIELDS, 8, 128), F32),
             v((CHUNKS, 2, 2, 8, 128), F32), v((CHUNKS, 2, 2, 8, 128), F32),
-            v((128, 12288), BF16), v((64, nc), BF16),
+            v((256, 1536), BF16), v((256, 1536), BF16), v((64, 3072), BF16), v((64, nc), BF16),
             v((nz, 2, 128), F32), v((2 * ny * nx, 8, nz * 32), F32),
             v((12, 8, 128), F32), v((12, 8, 128), F32), v((12, 8, 128), F32), v((12, 8, 128), F32),
             v((12, 8, 128), F32),
             v((PER, 14, 8, 128), F32), v((PER, 14, 8, 128), F32), v((PER, 14, 8, 128), F32),
             v((14, 8, 128), F32), v((14, 8, 128), F32), v((14, 8, 128), F32),
             v((2, 96, 128), F32),
-            pltpu.SemaphoreType.DMA((128,)), pltpu.SemaphoreType.DMA((128,)), pltpu.SemaphoreType.DMA((6,)),
+            pltpu.SemaphoreType.DMA((128,)), pltpu.SemaphoreType.DMA((128,)), pltpu.SemaphoreType.DMA((7,)),
         ]
-        hbm, smem = pl.BlockSpec(memory_space=pl.ANY), pl.BlockSpec(memory_space=pltpu.SMEM)
+        hbm = pl.BlockSpec(memory_space=pltpu.HBM)
         result = pl.pallas_call(
             functools.partial(kernel, ny, nx, nz),
             out_shape=jax.ShapeDtypeStruct((768, 128), F32),
-            in_specs=[hbm, hbm, hbm, smem, smem, hbm, hbm],
-            out_specs=hbm,
+            in_specs=[hbm] * 7,
+            out_specs=pl.BlockSpec(memory_space=pltpu.VMEM),
             scratch_shapes=scratch,
             compiler_params=pltpu.CompilerParams(
-                collective_id=0, has_side_effects=True, vmem_limit_bytes=48 * 1024 * 1024
+                collective_id=0, has_side_effects=True, vmem_limit_bytes=64 * 1024 * 1024
             ),
             name="schwarz",
         )(

time: 93.3 us -> 72.1 us (0.77)
  the two profiles are of different devices: /device:TPU:1 before, /device:TPU:3 now
where the time goes in v2:
time: 72.1 us; the launch traced here: 72 us
  Pallas kernels  70.2 us (97%)
  local copies, waits for them, and re-layouts  1.77 us (2%)
    pallas_call x1, Pallas kernels, step(): pl.pallas_call(functools.partial(kernel, ny, nx, nz), out_shape=jax.Shape...  70.2 us
    unnamed x1, local copies, waits for them, and re-layouts  1.77 us

profile of v2, /device:TPU:3, one launch (start us, length us, event | category | flops | bytes accessed | tf_op | source)
XLA Modules:
  0.0 72.0 jit_solution(1062033927582585089)
XLA Ops:
  0.0 70.2 %schwarz.1 = f32[768,128]{1,0:T(8,128)} custom-call(f32[768,128]{1,0:T(8,128)} %bitcast.7, f32[768,128]{1,0:T(8,128)} %bitcast.8, s32[32,128]{1,0:T(8,128)} %bitcast.9, f32[8]{0:T(128)} %stiffness_in.1, f32[8]{0:T(128)} %density_in.1, f32[3072,128]{1,0:T(8,128)} %bitcast.5, f32[32,16384]{1,0:T(8,128)} %cinv.1), custom_call_target="tpu_custom_call" | custom-call | tf_op jit(solution)/shard_map/schwarz/pallas_call | solution.py:623
  70.2 1.8 %copy.9 = f32[8,3,4,8,128]{4,3,2,1,0:T(8,128)} copy(f32[8,3,4,8,128]{4,3,2,1,0:T(8,128)} %bitcast.6) | data formatting | bytes 786432

commit v3 on v2

--- a/solution.py
+++ b/solution.py
@@ -39,7 +39,7 @@
 def kernel(
     ny, nx, nz, loads, iterate, classes, stiffness_in, density_in, basis, cinv, acc,
     it, ld, cls, stiffness, density, bas, ci, res, iys, iyr, ixs, ixr, izs, izr, cbox, czs, czr, box, ys, yr,
-    zs, zr, bh, bl, bf, c2, g1, g2, sbox, wbox, bbox, zw, zb, ga, gb, gc, za, zc, zd, vy,
+    zs, zr, bh, bl, bf, wide, c2, g1, g2, sbox, wbox, bbox, zw, zb, ga, gb, gc, za, zc, zd, vy,
     ss, rs, ls,
 ):
     gx, gy, gz = lax.axis_index("gx"), lax.axis_index("gy"), lax.axis_index("gz")
@@ -156,8 +156,8 @@
     peers = nz - 1 + nx * ny - 1 + 1 + across_gx.astype(I32) + across_gy.astype(I32)
     pl.semaphore_wait(barrier, peers)
 
+    it_y = exchange("gy", iys.at[0], iyr.at[1], iys.at[1], iyr.at[0])
     cls_y = exchange("gy", cbox.at[2:4, 2:6], cbox.at[10:12, 2:6], cbox.at[8:10, 2:6], cbox.at[0:2, 2:6])
-    it_y = exchange("gy", iys.at[0], iyr.at[1], iys.at[1], iyr.at[0])
     it_x = exchange("gx", ixs.at[0], ixr.at[1], ixs.at[1], ixr.at[0])
     it_z = exchange("gz", izs.at[0], izr.at[1], izs.at[1], izr.at[0])
 
@@ -214,6 +214,7 @@
 
     send_rows(0)
     send_rows(1)
+    send_rows(2)
 
     local[3].wait()
 
@@ -254,7 +255,6 @@
     fold = (iota((256, 128), 0) // 8 == iota((256, 128), 1)).astype(BF16)
     folded = jnp.dot(two(sums), fold, preferred_element_type=F32)
     coeff = folded[0:8] + folded[8:16]
-    unfold = (iota((128, 256), 0) == iota((128, 256), 1) // 8).astype(BF16)
 
     local[4].wait()
 
@@ -269,47 +269,6 @@
 
     cls_y()
     cls_x = exchange("gx", cbox.at[:, 2:4], cbox.at[:, 6:8], cbox.at[:, 4:6], cbox.at[:, 0:2])
-    cls_x()
-    low = jnp.zeros((8, 128), I32)
-    high = jnp.zeros((8, 128), I32)
-    for y in range(12):
-        mask = lane8 // 2 == y
-        low = jnp.where(mask, pltpu.roll(cbox[y], 2 * y, 1), low)
-        high = jnp.where(mask, pltpu.roll(cbox[y], 2 * y + 2, 1), high)
-    czs[0] = low
-    czs[1] = high
-    cls_z = exchange("gz", czs.at[0], czr.at[1], czs.at[1], czr.at[0])
-    cls_z()
-
-    def z_lanes(low, high, t, width):
-        odd = lane8 % 2 == 1
-        low, high = pltpu.roll(low, (128 - t) % 128, 1), pltpu.roll(high, (128 - t) % 128, 1)
-        inner = jnp.where(odd, low, high)
-        outer = jnp.where(odd, pltpu.roll(low, 1, 1), pltpu.roll(high, 127, 1))
-        zero = jnp.zeros_like(inner)
-        return jnp.where(lane8 < width, inner, zero) + pltpu.roll(jnp.where(lane8 < width, outer, zero), 64, 1)
-
-    def factors(shifted):
-        inside = shifted > 0
-        stiff = lookup(shifted - 1, stiffness)
-        mass = lookup(shifted - 1, density)
-        weight = jnp.where(inside, DAMPING / jnp.where(inside, 6.0 * stiff + mass - COUPLING * stiff, 1.0), 0.0)
-        return stiff, weight
-
-    def box_factors(y, carry):
-        stiff, weight = factors(cbox[y])
-        sbox[y] = stiff
-        wbox[y] = weight
-        bbox[y] = stiff * weight
-        spread = z_lanes(czr[0], czr[1], 2 * y, 2)
-        pair = spread + pltpu.roll(spread, 2, 1)
-        spread = pair + pltpu.roll(pair, 4, 1) + pltpu.roll(pair, 8, 1)
-        stiff, weight = factors(spread)
-        zw[y] = weight
-        zb[y] = stiff * weight
-        return carry
-
-    lax.fori_loop(0, 12, box_factors, 0, unroll=6)
 
     it_y()
     parts = []
@@ -351,12 +310,22 @@
         return carry
 
     lax.fori_loop(1, nz, start_line, 0)
-    send_rows(2)
     send_rows(3)
     for side in range(2):
         at = pl.ds(side * 7, 96, stride=8)
         res[at, :] = res[at, :] + vy[side]
 
+    cls_x()
+    low = jnp.zeros((8, 128), I32)
+    high = jnp.zeros((8, 128), I32)
+    for y in range(12):
+        mask = lane8 // 2 == y
+        low = jnp.where(mask, pltpu.roll(cbox[y], 2 * y, 1), low)
+        high = jnp.where(mask, pltpu.roll(cbox[y], 2 * y + 2, 1), high)
+    czs[0] = low
+    czs[1] = high
+    cls_z = exchange("gz", czs.at[0], czr.at[1], czs.at[1], czr.at[0])
+
     def own_rows(f, carry):
         for y in range(8):
             box[f, y + 2, 2:6] = res[pl.ds(f * 32 + y, 4, stride=8), :]
@@ -364,6 +333,39 @@
 
     lax.fori_loop(0, FIELDS, own_rows, 0, unroll=2)
     own_x = exchange("gx", box.at[:, 2:10, 2:4], box.at[:, 2:10, 6:8], box.at[:, 2:10, 4:6], box.at[:, 2:10, 0:2])
+
+
+    def z_lanes(low, high, t, width):
+        odd = lane8 % 2 == 1
+        low, high = pltpu.roll(low, (128 - t) % 128, 1), pltpu.roll(high, (128 - t) % 128, 1)
+        inner = jnp.where(odd, low, high)
+        outer = jnp.where(odd, pltpu.roll(low, 1, 1), pltpu.roll(high, 127, 1))
+        zero = jnp.zeros_like(inner)
+        return jnp.where(lane8 < width, inner, zero) + pltpu.roll(jnp.where(lane8 < width, outer, zero), 64, 1)
+
+    cls_z()
+
+    def factors(shifted):
+        inside = shifted > 0
+        stiff = lookup(shifted - 1, stiffness)
+        mass = lookup(shifted - 1, density)
+        weight = jnp.where(inside, DAMPING / jnp.where(inside, 6.0 * stiff + mass - COUPLING * stiff, 1.0), 0.0)
+        return stiff, weight
+
+    def box_factors(y, carry):
+        stiff, weight = factors(cbox[y])
+        sbox[y] = stiff
+        wbox[y] = weight
+        bbox[y] = stiff * weight
+        spread = z_lanes(czr[0], czr[1], 2 * y, 2)
+        pair = spread + pltpu.roll(spread, 2, 1)
+        spread = pair + pltpu.roll(pair, 4, 1) + pltpu.roll(pair, 8, 1)
+        stiff, weight = factors(spread)
+        zw[y] = weight
+        zb[y] = stiff * weight
+        return carry
+
+    lax.fori_loop(0, 12, box_factors, 0, unroll=6)
 
     res_x, res_z = {}, {}
 
@@ -522,60 +524,69 @@
 
     width = nz * 32
 
-    def times_block(b, total):
-        at = pl.ds(pl.multiple_of(b * width, width), width)
-        return total + lax.dot_general(two(g2[b]), c2[:, at], NT, preferred_element_type=F32)
+    def times_blocks(c, total):
+        def add(p, total):
+            x, y = other(p, -1)
+            b = block(x, y, c)
+            at = pl.ds(pl.multiple_of(b * width, width), width)
+            return total + lax.dot_general(two(g2[b]), c2[:, at], NT, preferred_element_type=F32)
+
+        return lax.fori_loop(0, nx * ny, add, total, unroll=nx * ny)
 
     def plane_arrives():
-        def arrive(p, total):
+        def arrive(p, carry):
             along_plane(p).wait_recv()
             to_twin(p).start()
-            x, y = other(p, -1)
-            return times_block(block(x, y, core), total)
-
-        return lax.fori_loop(1, nx * ny, arrive, times_block(block(px, py, core), jnp.zeros((16, 64), F32)))
+            return carry
+
+        lax.fori_loop(1, nx * ny, arrive, 0)
+        return times_blocks(core, jnp.zeros((16, 64), F32))
 
     def twins_arrive(total):
-        def arrive(p, total):
+        def arrive(p, carry):
             to_twin(p).wait_recv()
-            x, y = other(p, -1)
-            return times_block(block(x, y, 1 - core), total)
-
-        total = lax.fori_loop(0, nx * ny, arrive, total)
+            return carry
+
+        lax.fori_loop(0, nx * ny, arrive, 0)
+        total = times_blocks(1 - core, total)
         solved = quarters(total)
-        spread = jnp.dot(two(solved), unfold, preferred_element_type=F32)
-        spread = spread[0:8] + spread[8:16]
-        rows = jnp.broadcast_to(spread[:, None], (8, 8, 256)).reshape(64, 256)
-        hi, lo = halves(jnp.where(equal, rows, 0.0))
+        for j in range(32):
+            column = jnp.broadcast_to(solved[:, j : j + 1], (8, 128))
+            wide[j] = jnp.broadcast_to(column[:, None], (8, 8, 128))
 
         def correct(k, carry):
-            at = pl.ds(pl.multiple_of(k * 256, 256), 256)
-            v = jnp.dot(hi, bh[:, at], preferred_element_type=F32)
-            v = v + jnp.dot(lo, bh[:, at], preferred_element_type=F32)
-            v = v + jnp.dot(hi, bl[:, at], preferred_element_type=F32)
+            def add(j, sums):
+                parts = [bas[pl.ds(pl.multiple_of(j * 96 + k * 16 + i * 8, 8), 8), :] for i in range(2)]
+                out = []
+                for col in range(8):
+                    factor = wide[j, col]
+                    out += [sums[2 * col + i] + factor * parts[i] for i in range(2)]
+                return tuple(out)
+
+            sums = lax.fori_loop(0, 32, add, (zero8,) * 16, unroll=8)
             for col in range(8):
                 for i in range(2):
-                    rows = pl.ds(pl.multiple_of(col * 96 + (k * 2 + i) * 8, 8), 8)
-                    acc[rows, :] = acc[rows, :] + v[col * 8 : col * 8 + 8, i * 128 : i * 128 + 128]
-            return carry
-
-        lax.fori_loop(0, 6, correct, 0, unroll=6)
+                    rows = pl.ds(pl.multiple_of(col * 96 + k * 16 + i * 8, 8), 8)
+                    acc[rows, :] = acc[rows, :] + sums[2 * col + i]
+            return carry
+
+        lax.fori_loop(0, 6, correct, 0)
 
     rows_arrive(0)
     rows_arrive(1)
+    line_arrives()
+    rows_arrive(2)
+    rows_arrive(3)
     planes_arrive(0)
-    line_arrives()
     planes_arrive(1)
+    planes_arrive(2)
+    planes_arrive(3)
     sweeps(0)
-    rows_arrive(2)
+    total = plane_arrives()
     sweeps(1)
-    planes_arrive(2)
-    rows_arrive(3)
-    total = plane_arrives()
+    sweeps(2)
+    sweeps(3)
     twins_arrive(total)
-    sweeps(2)
-    planes_arrive(3)
-    sweeps(3)
 
     for sent in pending:
         sent()
@@ -610,7 +621,7 @@
             v((12, 8, 128), I32), v((2, 8, 128), I32), v((2, 8, 128), I32),
             v((FIELDS, 12, 8, 128), F32), v((2, FIELDS, 8, 128), F32), v((2, FIELDS, 8, 128), F32),
             v((CHUNKS, 2, 2, 8, 128), F32), v((CHUNKS, 2, 2, 8, 128), F32),
-            v((256, 1536), BF16), v((256, 1536), BF16), v((64, 3072), BF16), v((64, nc), BF16),
+            v((256, 1536), BF16), v((256, 1536), BF16), v((64, 3072), BF16), v((32, 8, 8, 128), F32), v((64, nc), BF16),
             v((nz, 2, 128), F32), v((2 * ny * nx, 8, nz * 32), F32),
             v((12, 8, 128), F32), v((12, 8, 128), F32), v((12, 8, 128), F32), v((12, 8, 128), F32),
             v((12, 8, 128), F32),

time: 72.1 us -> 67.5 us (0.936)
  the two profiles are of different devices: /device:TPU:3 before, /device:TPU:1 now
where the time goes in v3:
time: 67.5 us; the launch traced here: 67.2 us
  Pallas kernels  65.4 us (97%)
  local copies, waits for them, and re-layouts  1.77 us (3%)
    pallas_call x1, Pallas kernels, step(): pl.pallas_call(functools.partial(kernel, ny, nx, nz), out_shape=jax.Shape...  65.4 us
    unnamed x1, local copies, waits for them, and re-layouts  1.77 us

profile of v3, /device:TPU:1, one launch (start us, length us, event | category | flops | bytes accessed | tf_op | source)
XLA Modules:
  0.0 67.2 jit_solution(18121240021305348495)
XLA Ops:
  0.0 65.4 %schwarz.1 = f32[768,128]{1,0:T(8,128)} custom-call(f32[768,128]{1,0:T(8,128)} %bitcast.7, f32[768,128]{1,0:T(8,128)} %bitcast.8, s32[32,128]{1,0:T(8,128)} %bitcast.9, f32[8]{0:T(128)} %stiffness_in.1, f32[8]{0:T(128)} %density_in.1, f32[3072,128]{1,0:T(8,128)} %bitcast.5, f32[32,16384]{1,0:T(8,128)} %cinv.1), custom_call_target="tpu_custom_call" | custom-call | tf_op jit(solution)/shard_map/schwarz/pallas_call | solution.py:634
  65.4 1.8 %copy.9 = f32[8,3,4,8,128]{4,3,2,1,0:T(8,128)} copy(f32[8,3,4,8,128]{4,3,2,1,0:T(8,128)} %bitcast.6) | data formatting | bytes 786432

commit v4 on v3

--- a/solution.py
+++ b/solution.py
@@ -86,11 +86,8 @@
             )
         )
     ]
-    for copy in local:
-        copy.start()
-
-    for ref in (iyr, ixr, izr, cbox, czr, box, yr, zr):
-        ref[...] = jnp.zeros(ref.shape, ref.dtype)
+    for i in (0, 1, 5, 6, 2):
+        local[i].start()
 
     barrier = pltpu.get_barrier_semaphore()
     high_half = gy % 2
@@ -119,11 +116,42 @@
     pl.semaphore_signal(barrier, inc=1, device_id=twin, device_id_type=MESH)
 
     lane8 = iota((8, 128), 1)
-    sub8 = iota((8, 128), 0)
+    zero8 = jnp.zeros((8, 128), F32)
+
+    def clear(*views):
+        def store():
+            for ref, index in views:
+                view = ref.at[index]
+                view[...] = jnp.zeros(view.shape, ref.dtype)
+
+        return store
+
+    everything = slice(None)
+    for side in range(2):
+        layers = slice(10 * side, 10 * side + 2)
+        planes = slice(6 * side, 6 * side + 2)
+        missing = {axis: jnp.logical_not(step[1 + 2 * side]) for axis, step in steps.items()}
+        pl.when(missing["gy"])(
+            clear((iyr, side), (cbox, (layers, slice(2, 6))), (box, (everything, layers, slice(2, 6))))
+        )
+        pl.when(missing["gx"])(
+            clear((ixr, side), (cbox, (everything, planes)), (box, (everything, everything, planes)))
+        )
+        pl.when(missing["gz"])(clear((izr, side), (czr, side), (zr, (everything, side))))
 
     local[0].wait()
     iys[0] = it[pl.ds(0, 96, stride=8), :]
     iys[1] = it[pl.ds(7, 96, stride=8), :]
+
+    peers = nz - 1 + nx * ny - 1 + 1 + across_gx.astype(I32) + across_gy.astype(I32)
+    pl.semaphore_wait(barrier, peers)
+
+    it_y = exchange("gy", iys.at[0], iyr.at[1], iys.at[1], iyr.at[0])
+    local[1].wait()
+    for y in range(8):
+        cbox[y + 2, 2:6] = cls[pl.ds(y, 4, stride=8), :] + 1
+
+    cls_y = exchange("gy", cbox.at[2:4, 2:6], cbox.at[10:12, 2:6], cbox.at[8:10, 2:6], cbox.at[0:2, 2:6])
 
     def pack_iterate(f, carry):
         low, high = carry
@@ -137,14 +165,14 @@
             high = jnp.where(lane8 == t, pltpu.roll(v, t + 1, 1), high)
         return low, high
 
-    zero8 = jnp.zeros((8, 128), F32)
     low, high = lax.fori_loop(0, FIELDS, pack_iterate, (zero8, zero8), unroll=2)
     izs[0] = low
     izs[1] = high
-    local[1].wait()
-    for y in range(8):
-        cbox[y + 2, 2:6] = cls[pl.ds(y, 4, stride=8), :] + 1
-
+    it_x = exchange("gx", ixs.at[0], ixr.at[1], ixs.at[1], ixr.at[0])
+    it_z = exchange("gz", izs.at[0], izr.at[1], izs.at[1], izr.at[0])
+
+    for i in (3, 4):
+        local[i].start()
     acc[...] = it[...]
     for ref in (ga, gb, gc):
         ref[:, 0] = jnp.zeros((PER, 8, 128), F32)
@@ -152,14 +180,6 @@
     for ref in (za, zc, zd):
         ref[0] = zero8
         ref[13] = zero8
-
-    peers = nz - 1 + nx * ny - 1 + 1 + across_gx.astype(I32) + across_gy.astype(I32)
-    pl.semaphore_wait(barrier, peers)
-
-    it_y = exchange("gy", iys.at[0], iyr.at[1], iys.at[1], iyr.at[0])
-    cls_y = exchange("gy", cbox.at[2:4, 2:6], cbox.at[10:12, 2:6], cbox.at[8:10, 2:6], cbox.at[0:2, 2:6])
-    it_x = exchange("gx", ixs.at[0], ixr.at[1], ixs.at[1], ixr.at[0])
-    it_z = exchange("gz", izs.at[0], izr.at[1], izs.at[1], izr.at[0])
 
     local[5].wait()
     local[6].wait()
@@ -582,8 +602,8 @@
     planes_arrive(2)
     planes_arrive(3)
     sweeps(0)
+    sweeps(1)
     total = plane_arrives()
-    sweeps(1)
     sweeps(2)
     sweeps(3)
     twins_arrive(total)

time: 67.5 us -> 66.7 us (0.988)
  Pallas kernels: 65.4 us -> 64.7 us
    pallas_call x1, Pallas kernels: 65.4 us -> 64.7 us  [step(): pl.pallas_call(functools.partial(kernel, ny, nx, nz), out_shape=jax.Shape...]
where the time goes in v4:
time: 66.7 us; the launch traced here: 66.5 us
  Pallas kernels  64.7 us (97%)
  local copies, waits for them, and re-layouts  1.77 us (3%)
    pallas_call x1, Pallas kernels, step(): pl.pallas_call(functools.partial(kernel, ny, nx, nz), out_shape=jax.Shape...  64.7 us
    unnamed x1, local copies, waits for them, and re-layouts  1.77 us

profile of v4, /device:TPU:1, one launch (start us, length us, event | category | flops | bytes accessed | tf_op | source)
XLA Modules:
  0.0 66.5 jit_solution(5401798954916901010)
XLA Ops:
  0.0 64.7 %schwarz.1 = f32[768,128]{1,0:T(8,128)} custom-call(f32[768,128]{1,0:T(8,128)} %bitcast.7, f32[768,128]{1,0:T(8,128)} %bitcast.8, s32[32,128]{1,0:T(8,128)} %bitcast.9, f32[8]{0:T(128)} %stiffness_in.1, f32[8]{0:T(128)} %density_in.1, f32[3072,128]{1,0:T(8,128)} %bitcast.5, f32[32,16384]{1,0:T(8,128)} %cinv.1), custom_call_target="tpu_custom_call" | custom-call | tf_op jit(solution)/shard_map/schwarz/pallas_call | solution.py:654
  64.8 1.8 %copy.9 = f32[8,3,4,8,128]{4,3,2,1,0:T(8,128)} copy(f32[8,3,4,8,128]{4,3,2,1,0:T(8,128)} %bitcast.6) | data formatting | bytes 786432
